TPU v7x, 32 devices: a whole 2x2x4 slice. The times are simulated.
32 devices in a mesh: groups: 2 (over y), cubes: 16 (over z, x, core).
Axes of the slice: x: 2, y: 2, z: 4, core: 2. Of those that a mesh axis runs over, the one named last changes fastest.
Arguments:
- query_rows: bfloat16 [4096, 2560], P(('groups', 'cubes')), parts along dimension 0, may hold values from -8 to 8
- key_rows: bfloat16 [4096, 2560], P(('groups', 'cubes')), parts along dimension 0, may hold values from -9 to 9
- value_rows: bfloat16 [4096, 2560], P(('groups', 'cubes')), parts along dimension 0, may hold values from -6 to 6
- gate_logits: bfloat16 [4096, 40], P(('groups', 'cubes')), parts along dimension 0, may hold values from -6 to 6
- selection: int32 [64, 20, 8], P('groups'), parts along dimension 0, may hold values from 0 to 31, all different within a row; in each aligned block of 40 rows (0 to 39, 40 to 79, ..., all dimensions but the last counted through in order) at most 11 rows name the same one
- cube_ids: int32 [64], P('groups'), parts along dimension 0, may hold values from 0 to 31, each once
Outputs:
- mixed: bfloat16 [4096, 2560], P(('groups', 'cubes')), parts along dimension 0
There are 2 independent parts, one for each index of `groups`. A program takes and returns all parts, laid end to end along the dimension named above; each array names one. Nothing has to cross between parts.
Inputs may be any that keep to these rules, and one draw needn't show every extreme that they name: `selection`: each row of 8 names different cubes. Among the rows of one device (its 2 stored blocks with all 20 heads) no cube is named more than 11 times, a bound that some block reaches. `cube_ids`: each cube number appears once.
All inputs are finite; a program needn't handle non-finite values.
Results may differ from a plain program's by a relative error of at most 0.0047.
Values may be sent and summed in bfloat16 or wider, within the bound.
A program may use at most 128 MiB of HBM per device.

v0:
```python
import math

import jax
import jax.numpy as jnp
from jax import lax
from jax.sharding import PartitionSpec as P

CUBE = 64


NEG_START = -1e30


def block_partials(query_slots, pair_slots):
    head_size = query_slots.shape[-1]
    factor = 1.0 / math.sqrt(head_size)
    slot_keys = pair_slots[:, :, :head_size]
    slot_values = pair_slots[:, :, head_size:]
    scores = (
        jnp.einsum("sqd,skd->sqk", query_slots, slot_keys, preferred_element_type=jnp.float32)
        * factor
    )
    slot_max = jnp.max(scores, axis=2)
    weights = jnp.exp(scores - slot_max[:, :, None])
    slot_total = jnp.sum(weights, axis=2)
    numerator = jnp.einsum(
        "sqk,skd->sqd",
        weights.astype(jnp.bfloat16),
        slot_values,
        preferred_element_type=jnp.float32,
    )
    return (numerator, slot_max, slot_total)


def merge_slots(state, results, slot_group):
    numerator, running_max, totals = state
    slot_numerator, slot_max, slot_total = results
    group_count = numerator.shape[0]
    slot_count = slot_group.shape[0]
    member = slot_group[:, None] == jnp.arange(group_count, dtype=jnp.int32)[None, :]
    is_valid = slot_group >= 0
    group_max = jnp.max(jnp.where(member[:, :, None], slot_max[:, None, :], -jnp.inf), axis=0)
    new_max = jnp.maximum(running_max, group_max)
    slot_base = jnp.take(new_max, jnp.maximum(slot_group, 0), axis=0)
    slot_weight = jnp.exp(jnp.where(is_valid[:, None], slot_max - slot_base, -jnp.inf))
    onehot = member.astype(jnp.float32).T
    weighted = (slot_weight[:, :, None] * slot_numerator).reshape(slot_count, -1)
    added_numerator = jnp.dot(onehot, weighted, precision=lax.Precision.HIGHEST).reshape(
        numerator.shape
    )
    added_total = jnp.dot(onehot, slot_weight * slot_total, precision=lax.Precision.HIGHEST)
    decay_factor = jnp.exp(running_max - new_max)
    return (
        numerator * decay_factor[:, :, None] + added_numerator,
        new_max,
        totals * decay_factor + added_total,
    )


def body(query_rows, key_rows, value_rows, gate_logits, selection, cube_ids):
    device_count = lax.axis_size("cubes")
    token_count = query_rows.shape[0]
    feature_width = query_rows.shape[1]
    head_count = gate_logits.shape[1] // 2
    head_size = feature_width // head_count
    local_cubes = token_count // CUBE
    total_cubes = cube_ids.shape[0]
    picks_each = selection.shape[2]
    depth_rounds = max(2, head_count * picks_each // device_count + 1)
    request_count = local_cubes * head_count * picks_each
    factor = 1.0 / math.sqrt(head_size)
    self_index = lax.axis_index("cubes")
    pooled_keys = jnp.mean(
        key_rows.reshape(local_cubes, CUBE, feature_width), axis=1, dtype=jnp.float32
    ).astype(jnp.bfloat16)
    pooled_values = jnp.mean(
        value_rows.reshape(local_cubes, CUBE, feature_width), axis=1, dtype=jnp.float32
    ).astype(jnp.bfloat16)
    query_heads = query_rows.reshape(token_count, head_count, head_size)
    start_state = (
        jnp.zeros((head_count, token_count, head_size), jnp.float32),
        jnp.full((head_count, token_count), NEG_START, jnp.float32),
        jnp.zeros((head_count, token_count), jnp.float32),
    )
    numerator, running_max, totals = start_state
    piece_keys = lax.all_gather(pooled_keys, "cubes", axis=0, tiled=True)
    piece_values = lax.all_gather(pooled_values, "cubes", axis=0, tiled=True)
    piece_rows = piece_keys.shape[0]
    scores = (
        jnp.einsum(
            "thd,jhd->htj",
            query_heads,
            piece_keys.reshape(piece_rows, head_count, head_size),
            preferred_element_type=jnp.float32,
        )
        * factor
    )
    new_max = jnp.maximum(running_max, jnp.max(scores, axis=2))
    weights = jnp.exp(scores - new_max[:, :, None])
    added = jnp.einsum(
        "htj,jhd->htd",
        weights.astype(jnp.bfloat16),
        piece_values.reshape(piece_rows, head_count, head_size),
        preferred_element_type=jnp.float32,
    )
    numerator = added
    totals = jnp.sum(weights, axis=2)
    coarse = jnp.transpose(numerator / totals[:, :, None], (1, 0, 2))
    cube_range = jnp.arange(total_cubes, dtype=jnp.int32)
    position = jnp.sum(
        jnp.where(cube_ids[None, :] == cube_range[:, None], cube_range[None, :], 0), axis=1
    )
    targets = jnp.take(position, selection.reshape(-1)).reshape(device_count, request_count)
    request_range = jnp.arange(request_count, dtype=jnp.int32)
    request_group = request_range // picks_each
    request_head = request_group % head_count
    round_range = jnp.arange(depth_rounds, dtype=jnp.int32)
    own_targets = lax.dynamic_index_in_dim(targets, self_index, 0, keepdims=False)
    same_target = own_targets[:, None] == cube_range[None, :]
    running_count = jnp.cumsum(same_target.astype(jnp.int32), axis=0)
    own_rank = jnp.sum(jnp.where(same_target, running_count, 0), axis=1) - 1
    chosen_round = same_target[None, :, :] & (own_rank[None, :, None] == round_range[:, None, None])
    wanted_all = jnp.sum(jnp.where(chosen_round, request_group[None, :, None] + 1, 0), axis=1) - 1
    own_cubes = self_index * local_cubes + jnp.arange(local_cubes, dtype=jnp.int32)
    hit_mine = targets[:, :, None] == own_cubes[None, None, :]
    mine_rank = jnp.cumsum(hit_mine.astype(jnp.int32), axis=1) - 1
    round_hit = hit_mine[None] & (mine_rank[None] == round_range[:, None, None, None])
    incoming_all = (
        jnp.sum(jnp.where(round_hit, request_head[None, None, :, None] + 1, 0), axis=2) - 1
    )
    query_groups = (
        query_rows.reshape(local_cubes, CUBE, head_count, head_size)
        .transpose(0, 2, 1, 3)
        .reshape(local_cubes * head_count, CUBE, head_size)
    )
    pair_blocks = jnp.concatenate(
        (
            key_rows.reshape(local_cubes, CUBE, head_count, head_size),
            value_rows.reshape(local_cubes, CUBE, head_count, head_size),
        ),
        axis=3,
    )
    pair_groups = pair_blocks.transpose(0, 2, 1, 3).reshape(
        local_cubes * head_count, CUBE, 2 * head_size
    )
    base_group = head_count * jnp.arange(local_cubes, dtype=jnp.int32)

    def held_pairs(incoming):
        source = (jnp.maximum(incoming, 0) + base_group[None, :]).reshape(-1)
        picked = jnp.take(pair_groups, source, axis=0)
        return jnp.where(
            (incoming >= 0).reshape(-1)[:, None, None], picked, jnp.zeros((), jnp.bfloat16)
        )

    def asked_queries(wanted):
        picked = jnp.take(query_groups, jnp.maximum(wanted, 0), axis=0)
        return jnp.where((wanted >= 0)[:, None, None], picked, jnp.zeros((), jnp.bfloat16))

    def one_round(state, tables):
        wanted, incoming = tables
        arrived = lax.all_to_all(
            held_pairs(incoming), "cubes", split_axis=0, concat_axis=0, tiled=True
        )
        results = block_partials(asked_queries(wanted), arrived)
        return (merge_slots(state, results, wanted), None)

    group_count = local_cubes * head_count
    start_state = (
        jnp.zeros((group_count, CUBE, head_size), jnp.float32),
        jnp.full((group_count, CUBE), NEG_START, jnp.float32),
        jnp.zeros((group_count, CUBE), jnp.float32),
    )
    final_state, unused = lax.scan(one_round, start_state, (wanted_all, incoming_all))
    numerator, running_max, totals = final_state
    fine_groups = numerator / totals[:, :, None]
    fine = (
        fine_groups.reshape(local_cubes, head_count, CUBE, head_size)
        .transpose(0, 2, 1, 3)
        .reshape(token_count, head_count, head_size)
    )
    gates = jax.nn.sigmoid(gate_logits.astype(jnp.float32))
    mixed = gates[:, :head_count, None] * coarse + gates[:, head_count:, None] * fine
    return mixed.reshape(token_count, feature_width).astype(jnp.bfloat16)


def solution(mesh):
    placed = (
        P(("groups", "cubes"), None),
        P(("groups", "cubes"), None),
        P(("groups", "cubes"), None),
        P(("groups", "cubes"), None),
        P("groups", None, None),
        P("groups"),
    )
    return jax.shard_map(
        body, mesh=mesh, in_specs=placed, out_specs=P(("groups", "cubes"), None), check_vma=False
    )
```

profile of v0, /device:TPU:0, one launch (start us, length us, event | category | flops | bytes accessed | tf_op | source)
XLA Modules:
  0.0 513.2 jit_solution(15837783295440268176)
XLA Ops:
  2.8 4.5 compare_select_fusion.3
  9.5 15.6 %select_select_fusion.1 = s32[5120]{0:T(1024)S(1)} fusion(pred[5120]{0:T(1024)(128)(4,1)S(1)} %get-tuple-element.141, pred[5120]{0:T(1024)(128)(4,1)S(1)} %get-tuple-element.140, pred[5120]{0:T(1024)(128)(4,1)S(1)} %get-tuple-element.139, pred[5120]{0:T(1024)(128)(4,1)S(1)} %get-tuple-element.138, pred[5120]{0:T(1024)(128)(4,1)S(1)} %get-tuple-element.137, ...), kind=kLoop, calls=%fused_computation.125 | loop fusion | flops 128000 | bytes 169060 | tf_op jit(solution)/shard_map/jit(_take)/gather | solution.py:113
  32.9 433.4 %while.16 = (s32[]{:T(128)}, f32[40,64,128]{2,0,1:T(8,128)S(1)}, f32[40,64]{1,0:T(8,128)S(1)}, f32[40,64]{1,0:T(8,128)S(1)}, s32[11,32]{1,0:T(8,128)S(1)}, /*ind...) while((s32[]{:T(128)}, f32[40,64,128]{2,0,1:T(8,128)S(1)}, ...), condition=%wide.region_16.17_spmd.clone.clone, body=%wide.region_12.16_spmd.clone.clone.sunk | while | flops 197712672 | bytes 22294940 | solution.py:173
  33.6 1.9 gather_fusion
  36.8 7.4 %all-to-all-start = ((bf16[32,64,256]{2,1,0:T(8,128)(2,1)}), bf16[32,64,256]{2,1,0:T(8,128)(2,1)S(1)}, u32[]{:S(2)}, u32[]{:S(2)}) async-start(bf16[32,64,256]{2,1,0:T(8,128)(2,1)} %select_select_fusion.3), calls=%async_computation | async-start | bytes 2097152 | tf_op jit(solution)/shard_map/while/body/eval_jaxpr/all_to_all | solution.py:161
  45.7 21.4 %all-to-all-done = bf16[32,64,256]{2,1,0:T(8,128)(2,1)S(1)} async-done(((bf16[32,64,256]{2,1,0:T(8,128)(2,1)}), bf16[32,64,256]{2,1,0:T(8,128)(2,1)S(1)}, u32[]{:S(2)}, u32[]{:S(2)}) %all-to-all-start) | async-done | bytes 1048608 | tf_op jit(solution)/shard_map/while/body/eval_jaxpr/all_to_all | solution.py:161
  70.9 1.8 convolution_add_fusion.4
  73.5 1.9 gather_fusion
  76.6 6.9 %all-to-all-start = ((bf16[32,64,256]{2,1,0:T(8,128)(2,1)}), bf16[32,64,256]{2,1,0:T(8,128)(2,1)S(1)}, u32[]{:S(2)}, u32[]{:S(2)}) async-start(bf16[32,64,256]{2,1,0:T(8,128)(2,1)} %select_select_fusion.3), calls=%async_computation | async-start | bytes 2097152 | tf_op jit(solution)/shard_map/while/body/eval_jaxpr/all_to_all | solution.py:161
  85.1 21.4 %all-to-all-done = bf16[32,64,256]{2,1,0:T(8,128)(2,1)S(1)} async-done(((bf16[32,64,256]{2,1,0:T(8,128)(2,1)}), bf16[32,64,256]{2,1,0:T(8,128)(2,1)S(1)}, u32[]{:S(2)}, u32[]{:S(2)}) %all-to-all-start) | async-done | bytes 1048608 | tf_op jit(solution)/shard_map/while/body/eval_jaxpr/all_to_all | solution.py:161
  110.2 1.8 convolution_add_fusion.4
  112.8 1.9 gather_fusion
  116.0 6.9 %all-to-all-start = ((bf16[32,64,256]{2,1,0:T(8,128)(2,1)}), bf16[32,64,256]{2,1,0:T(8,128)(2,1)S(1)}, u32[]{:S(2)}, u32[]{:S(2)}) async-start(bf16[32,64,256]{2,1,0:T(8,128)(2,1)} %select_select_fusion.3), calls=%async_computation | async-start | bytes 2097152 | tf_op jit(solution)/shard_map/while/body/eval_jaxpr/all_to_all | solution.py:161
  124.4 21.4 %all-to-all-done = bf16[32,64,256]{2,1,0:T(8,128)(2,1)S(1)} async-done(((bf16[32,64,256]{2,1,0:T(8,128)(2,1)}), bf16[32,64,256]{2,1,0:T(8,128)(2,1)S(1)}, u32[]{:S(2)}, u32[]{:S(2)}) %all-to-all-start) | async-done | bytes 1048608 | tf_op jit(solution)/shard_map/while/body/eval_jaxpr/all_to_all | solution.py:161
  149.6 1.8 convolution_add_fusion.4
  152.2 1.9 gather_fusion
  155.4 6.9 %all-to-all-start = ((bf16[32,64,256]{2,1,0:T(8,128)(2,1)}), bf16[32,64,256]{2,1,0:T(8,128)(2,1)S(1)}, u32[]{:S(2)}, u32[]{:S(2)}) async-start(bf16[32,64,256]{2,1,0:T(8,128)(2,1)} %select_select_fusion.3), calls=%async_computation | async-start | bytes 2097152 | tf_op jit(solution)/shard_map/while/body/eval_jaxpr/all_to_all | solution.py:161
  163.8 21.4 %all-to-all-done = bf16[32,64,256]{2,1,0:T(8,128)(2,1)S(1)} async-done(((bf16[32,64,256]{2,1,0:T(8,128)(2,1)}), bf16[32,64,256]{2,1,0:T(8,128)(2,1)S(1)}, u32[]{:S(2)}, u32[]{:S(2)}) %all-to-all-start) | async-done | bytes 1048608 | tf_op jit(solution)/shard_map/while/body/eval_jaxpr/all_to_all | solution.py:161
  189.0 1.8 convolution_add_fusion.4
  191.6 1.9 gather_fusion
  194.7 6.9 %all-to-all-start = ((bf16[32,64,256]{2,1,0:T(8,128)(2,1)}), bf16[32,64,256]{2,1,0:T(8,128)(2,1)S(1)}, u32[]{:S(2)}, u32[]{:S(2)}) async-start(bf16[32,64,256]{2,1,0:T(8,128)(2,1)} %select_select_fusion.3), calls=%async_computation | async-start | bytes 2097152 | tf_op jit(solution)/shard_map/while/body/eval_jaxpr/all_to_all | solution.py:161
  203.1 21.4 %all-to-all-done = bf16[32,64,256]{2,1,0:T(8,128)(2,1)S(1)} async-done(((bf16[32,64,256]{2,1,0:T(8,128)(2,1)}), bf16[32,64,256]{2,1,0:T(8,128)(2,1)S(1)}, u32[]{:S(2)}, u32[]{:S(2)}) %all-to-all-start) | async-done | bytes 1048608 | tf_op jit(solution)/shard_map/while/body/eval_jaxpr/all_to_all | solution.py:161
  228.3 1.8 convolution_add_fusion.4
  230.9 1.9 gather_fusion
  234.1 6.9 %all-to-all-start = ((bf16[32,64,256]{2,1,0:T(8,128)(2,1)}), bf16[32,64,256]{2,1,0:T(8,128)(2,1)S(1)}, u32[]{:S(2)}, u32[]{:S(2)}) async-start(bf16[32,64,256]{2,1,0:T(8,128)(2,1)} %select_select_fusion.3), calls=%async_computation | async-start | bytes 2097152 | tf_op jit(solution)/shard_map/while/body/eval_jaxpr/all_to_all | solution.py:161
  242.5 21.4 %all-to-all-done = bf16[32,64,256]{2,1,0:T(8,128)(2,1)S(1)} async-done(((bf16[32,64,256]{2,1,0:T(8,128)(2,1)}), bf16[32,64,256]{2,1,0:T(8,128)(2,1)S(1)}, u32[]{:S(2)}, u32[]{:S(2)}) %all-to-all-start) | async-done | bytes 1048608 | tf_op jit(solution)/shard_map/while/body/eval_jaxpr/all_to_all | solution.py:161
  267.7 1.8 convolution_add_fusion.4
  270.3 1.9 gather_fusion
  273.4 6.9 %all-to-all-start = ((bf16[32,64,256]{2,1,0:T(8,128)(2,1)}), bf16[32,64,256]{2,1,0:T(8,128)(2,1)S(1)}, u32[]{:S(2)}, u32[]{:S(2)}) async-start(bf16[32,64,256]{2,1,0:T(8,128)(2,1)} %select_select_fusion.3), calls=%async_computation | async-start | bytes 2097152 | tf_op jit(solution)/shard_map/while/body/eval_jaxpr/all_to_all | solution.py:161
  281.9 21.4 %all-to-all-done = bf16[32,64,256]{2,1,0:T(8,128)(2,1)S(1)} async-done(((bf16[32,64,256]{2,1,0:T(8,128)(2,1)}), bf16[32,64,256]{2,1,0:T(8,128)(2,1)S(1)}, u32[]{:S(2)}, u32[]{:S(2)}) %all-to-all-start) | async-done | bytes 1048608 | tf_op jit(solution)/shard_map/while/body/eval_jaxpr/all_to_all | solution.py:161
  309.6 1.9 gather_fusion
  312.8 6.9 %all-to-all-start = ((bf16[32,64,256]{2,1,0:T(8,128)(2,1)}), bf16[32,64,256]{2,1,0:T(8,128)(2,1)S(1)}, u32[]{:S(2)}, u32[]{:S(2)}) async-start(bf16[32,64,256]{2,1,0:T(8,128)(2,1)} %select_select_fusion.3), calls=%async_computation | async-start | bytes 2097152 | tf_op jit(solution)/shard_map/while/body/eval_jaxpr/all_to_all | solution.py:161
  321.2 21.4 %all-to-all-done = bf16[32,64,256]{2,1,0:T(8,128)(2,1)S(1)} async-done(((bf16[32,64,256]{2,1,0:T(8,128)(2,1)}), bf16[32,64,256]{2,1,0:T(8,128)(2,1)S(1)}, u32[]{:S(2)}, u32[]{:S(2)}) %all-to-all-start) | async-done | bytes 1048608 | tf_op jit(solution)/shard_map/while/body/eval_jaxpr/all_to_all | solution.py:161
  346.4 1.8 convolution_add_fusion.4
  349.0 1.9 gather_fusion
  352.1 6.9 %all-to-all-start = ((bf16[32,64,256]{2,1,0:T(8,128)(2,1)}), bf16[32,64,256]{2,1,0:T(8,128)(2,1)S(1)}, u32[]{:S(2)}, u32[]{:S(2)}) async-start(bf16[32,64,256]{2,1,0:T(8,128)(2,1)} %select_select_fusion.3), calls=%async_computation | async-start | bytes 2097152 | tf_op jit(solution)/shard_map/while/body/eval_jaxpr/all_to_all | solution.py:161
  360.6 21.4 %all-to-all-done = bf16[32,64,256]{2,1,0:T(8,128)(2,1)S(1)} async-done(((bf16[32,64,256]{2,1,0:T(8,128)(2,1)}), bf16[32,64,256]{2,1,0:T(8,128)(2,1)S(1)}, u32[]{:S(2)}, u32[]{:S(2)}) %all-to-all-start) | async-done | bytes 1048608 | tf_op jit(solution)/shard_map/while/body/eval_jaxpr/all_to_all | solution.py:161
  385.7 1.8 convolution_add_fusion.4
  388.3 1.9 gather_fusion
  391.5 6.9 %all-to-all-start = ((bf16[32,64,256]{2,1,0:T(8,128)(2,1)}), bf16[32,64,256]{2,1,0:T(8,128)(2,1)S(1)}, u32[]{:S(2)}, u32[]{:S(2)}) async-start(bf16[32,64,256]{2,1,0:T(8,128)(2,1)} %select_select_fusion.3), calls=%async_computation | async-start | bytes 2097152 | tf_op jit(solution)/shard_map/while/body/eval_jaxpr/all_to_all | solution.py:161
  399.9 21.4 %all-to-all-done = bf16[32,64,256]{2,1,0:T(8,128)(2,1)S(1)} async-done(((bf16[32,64,256]{2,1,0:T(8,128)(2,1)}), bf16[32,64,256]{2,1,0:T(8,128)(2,1)S(1)}, u32[]{:S(2)}, u32[]{:S(2)}) %all-to-all-start) | async-done | bytes 1048608 | tf_op jit(solution)/shard_map/while/body/eval_jaxpr/all_to_all | solution.py:161
  425.1 1.8 convolution_add_fusion.4
  427.7 1.9 gather_fusion
  430.8 6.9 %all-to-all-start = ((bf16[32,64,256]{2,1,0:T(8,128)(2,1)}), bf16[32,64,256]{2,1,0:T(8,128)(2,1)S(1)}, u32[]{:S(2)}, u32[]{:S(2)}) async-start(bf16[32,64,256]{2,1,0:T(8,128)(2,1)} %select_select_fusion.3), calls=%async_computation | async-start | bytes 2097152 | tf_op jit(solution)/shard_map/while/body/eval_jaxpr/all_to_all | solution.py:161
  439.3 21.4 %all-to-all-done = bf16[32,64,256]{2,1,0:T(8,128)(2,1)S(1)} async-done(((bf16[32,64,256]{2,1,0:T(8,128)(2,1)}), bf16[32,64,256]{2,1,0:T(8,128)(2,1)S(1)}, u32[]{:S(2)}, u32[]{:S(2)}) %all-to-all-start) | async-done | bytes 1048608 | tf_op jit(solution)/shard_map/while/body/eval_jaxpr/all_to_all | solution.py:161
  464.4 1.8 convolution_add_fusion.4
  469.6 23.3 %all-gather = bf16[16,2,2560]{2,1,0:T(2,128)(2,1)S(1)} all-gather(bf16[1,2,2560]{2,1,0:T(2,128)(2,1)S(1)} %fusion.37), channel_id=1, replica_groups=mesh['groups'=2,'cubes'=16] {'cubes'}, dimensions={0}, use_global_device_ids=true | all-gather | bytes 174080 | tf_op jit(solution)/shard_map/all_gather | solution.py:86
  493.5 18.0 %all-gather.1 = bf16[16,2,2560]{2,1,0:T(2,128)(2,1)S(1)} all-gather(bf16[1,2,2560]{2,1,0:T(2,128)(2,1)S(1)} %fusion.38), channel_id=1, replica_groups=mesh['groups'=2,'cubes'=16] {'cubes'}, dimensions={0}, use_global_device_ids=true | all-gather | bytes 174080 | tf_op jit(solution)/shard_map/all_gather | solution.py:87
  (541 shorter events, 98.1 us)
Async XLA Ops:
  2.6 27.3 %copy-start.4 = (bf16[128,2560]{1,0:T(8,128)(2,1)S(1)}, bf16[128,2560]{1,0:T(8,128)(2,1)}, u32[]{:S(2)}) copy-start(bf16[128,2560]{1,0:T(8,128)(2,1)} %param.9) | copy-start | bytes 1966084
  25.4 4.9 copy-start.6
  32.9 11.3 %copy-start = (bf16[40,64,128]{2,1,0:T(8,128)(2,1)}, bf16[40,64,128]{2,1,0:T(8,128)(2,1)S(1)}, u32[]{:S(2)}) copy-start(bf16[40,64,128]{2,1,0:T(8,128)(2,1)S(1)} %get-tuple-element.288) | copy-start | bytes 1966084 | tf_op jit(solution)/shard_map/while
  33.0 12.7 %copy-start.11 = (s32[11,32]{1,0:T(8,128)}, s32[11,32]{1,0:T(8,128)S(1)}, u32[]{:S(2)}) copy-start(s32[11,32]{1,0:T(8,128)S(1)} %get-tuple-element.287) | copy-start | bytes 4228 | tf_op jit(solution)/shard_map/while
  36.8 30.3 %all-to-all-start = ((bf16[32,64,256]{2,1,0:T(8,128)(2,1)}), bf16[32,64,256]{2,1,0:T(8,128)(2,1)S(1)}, u32[]{:S(2)}, u32[]{:S(2)}) async-start(bf16[32,64,256]{2,1,0:T(8,128)(2,1)} %select_select_fusion.3), calls=%async_computation | async-start | bytes 2097152 | tf_op jit(solution)/shard_map/while/body/eval_jaxpr/all_to_all | solution.py:161
  70.9 1.9 copy-start.1
  72.8 10.8 %copy-start = (bf16[40,64,128]{2,1,0:T(8,128)(2,1)}, bf16[40,64,128]{2,1,0:T(8,128)(2,1)S(1)}, u32[]{:S(2)}) copy-start(bf16[40,64,128]{2,1,0:T(8,128)(2,1)S(1)} %get-tuple-element.288) | copy-start | bytes 1966084 | tf_op jit(solution)/shard_map/while
  72.8 12.2 %copy-start.11 = (s32[11,32]{1,0:T(8,128)}, s32[11,32]{1,0:T(8,128)S(1)}, u32[]{:S(2)}) copy-start(s32[11,32]{1,0:T(8,128)S(1)} %get-tuple-element.287) | copy-start | bytes 4228 | tf_op jit(solution)/shard_map/while
  76.6 29.8 %all-to-all-start = ((bf16[32,64,256]{2,1,0:T(8,128)(2,1)}), bf16[32,64,256]{2,1,0:T(8,128)(2,1)S(1)}, u32[]{:S(2)}, u32[]{:S(2)}) async-start(bf16[32,64,256]{2,1,0:T(8,128)(2,1)} %select_select_fusion.3), calls=%async_computation | async-start | bytes 2097152 | tf_op jit(solution)/shard_map/while/body/eval_jaxpr/all_to_all | solution.py:161
  112.1 10.8 %copy-start = (bf16[40,64,128]{2,1,0:T(8,128)(2,1)}, bf16[40,64,128]{2,1,0:T(8,128)(2,1)S(1)}, u32[]{:S(2)}) copy-start(bf16[40,64,128]{2,1,0:T(8,128)(2,1)S(1)} %get-tuple-element.288) | copy-start | bytes 1966084 | tf_op jit(solution)/shard_map/while
  112.2 12.2 %copy-start.11 = (s32[11,32]{1,0:T(8,128)}, s32[11,32]{1,0:T(8,128)S(1)}, u32[]{:S(2)}) copy-start(s32[11,32]{1,0:T(8,128)S(1)} %get-tuple-element.287) | copy-start | bytes 4228 | tf_op jit(solution)/shard_map/while
  116.0 29.8 %all-to-all-start = ((bf16[32,64,256]{2,1,0:T(8,128)(2,1)}), bf16[32,64,256]{2,1,0:T(8,128)(2,1)S(1)}, u32[]{:S(2)}, u32[]{:S(2)}) async-start(bf16[32,64,256]{2,1,0:T(8,128)(2,1)} %select_select_fusion.3), calls=%async_computation | async-start | bytes 2097152 | tf_op jit(solution)/shard_map/while/body/eval_jaxpr/all_to_all | solution.py:161
  149.6 1.9 copy-start.1
  151.5 10.8 %copy-start = (bf16[40,64,128]{2,1,0:T(8,128)(2,1)}, bf16[40,64,128]{2,1,0:T(8,128)(2,1)S(1)}, u32[]{:S(2)}) copy-start(bf16[40,64,128]{2,1,0:T(8,128)(2,1)S(1)} %get-tuple-element.288) | copy-start | bytes 1966084 | tf_op jit(solution)/shard_map/while
  151.5 12.2 %copy-start.11 = (s32[11,32]{1,0:T(8,128)}, s32[11,32]{1,0:T(8,128)S(1)}, u32[]{:S(2)}) copy-start(s32[11,32]{1,0:T(8,128)S(1)} %get-tuple-element.287) | copy-start | bytes 4228 | tf_op jit(solution)/shard_map/while
  155.4 29.8 %all-to-all-start = ((bf16[32,64,256]{2,1,0:T(8,128)(2,1)}), bf16[32,64,256]{2,1,0:T(8,128)(2,1)S(1)}, u32[]{:S(2)}, u32[]{:S(2)}) async-start(bf16[32,64,256]{2,1,0:T(8,128)(2,1)} %select_select_fusion.3), calls=%async_computation | async-start | bytes 2097152 | tf_op jit(solution)/shard_map/while/body/eval_jaxpr/all_to_all | solution.py:161
  188.9 1.9 copy-start.1
  190.9 10.8 %copy-start = (bf16[40,64,128]{2,1,0:T(8,128)(2,1)}, bf16[40,64,128]{2,1,0:T(8,128)(2,1)S(1)}, u32[]{:S(2)}) copy-start(bf16[40,64,128]{2,1,0:T(8,128)(2,1)S(1)} %get-tuple-element.288) | copy-start | bytes 1966084 | tf_op jit(solution)/shard_map/while
  190.9 12.2 %copy-start.11 = (s32[11,32]{1,0:T(8,128)}, s32[11,32]{1,0:T(8,128)S(1)}, u32[]{:S(2)}) copy-start(s32[11,32]{1,0:T(8,128)S(1)} %get-tuple-element.287) | copy-start | bytes 4228 | tf_op jit(solution)/shard_map/while
  194.7 29.8 %all-to-all-start = ((bf16[32,64,256]{2,1,0:T(8,128)(2,1)}), bf16[32,64,256]{2,1,0:T(8,128)(2,1)S(1)}, u32[]{:S(2)}, u32[]{:S(2)}) async-start(bf16[32,64,256]{2,1,0:T(8,128)(2,1)} %select_select_fusion.3), calls=%async_computation | async-start | bytes 2097152 | tf_op jit(solution)/shard_map/while/body/eval_jaxpr/all_to_all | solution.py:161
  228.3 1.9 copy-start.1
  230.2 10.8 %copy-start = (bf16[40,64,128]{2,1,0:T(8,128)(2,1)}, bf16[40,64,128]{2,1,0:T(8,128)(2,1)S(1)}, u32[]{:S(2)}) copy-start(bf16[40,64,128]{2,1,0:T(8,128)(2,1)S(1)} %get-tuple-element.288) | copy-start | bytes 1966084 | tf_op jit(solution)/shard_map/while
  230.2 12.2 %copy-start.11 = (s32[11,32]{1,0:T(8,128)}, s32[11,32]{1,0:T(8,128)S(1)}, u32[]{:S(2)}) copy-start(s32[11,32]{1,0:T(8,128)S(1)} %get-tuple-element.287) | copy-start | bytes 4228 | tf_op jit(solution)/shard_map/while
  234.1 29.8 %all-to-all-start = ((bf16[32,64,256]{2,1,0:T(8,128)(2,1)}), bf16[32,64,256]{2,1,0:T(8,128)(2,1)S(1)}, u32[]{:S(2)}, u32[]{:S(2)}) async-start(bf16[32,64,256]{2,1,0:T(8,128)(2,1)} %select_select_fusion.3), calls=%async_computation | async-start | bytes 2097152 | tf_op jit(solution)/shard_map/while/body/eval_jaxpr/all_to_all | solution.py:161
  267.6 1.9 copy-start.1
  269.6 10.8 %copy-start = (bf16[40,64,128]{2,1,0:T(8,128)(2,1)}, bf16[40,64,128]{2,1,0:T(8,128)(2,1)S(1)}, u32[]{:S(2)}) copy-start(bf16[40,64,128]{2,1,0:T(8,128)(2,1)S(1)} %get-tuple-element.288) | copy-start | bytes 1966084 | tf_op jit(solution)/shard_map/while
  269.6 12.2 %copy-start.11 = (s32[11,32]{1,0:T(8,128)}, s32[11,32]{1,0:T(8,128)S(1)}, u32[]{:S(2)}) copy-start(s32[11,32]{1,0:T(8,128)S(1)} %get-tuple-element.287) | copy-start | bytes 4228 | tf_op jit(solution)/shard_map/while
  273.4 29.8 %all-to-all-start = ((bf16[32,64,256]{2,1,0:T(8,128)(2,1)}), bf16[32,64,256]{2,1,0:T(8,128)(2,1)S(1)}, u32[]{:S(2)}, u32[]{:S(2)}) async-start(bf16[32,64,256]{2,1,0:T(8,128)(2,1)} %select_select_fusion.3), calls=%async_computation | async-start | bytes 2097152 | tf_op jit(solution)/shard_map/while/body/eval_jaxpr/all_to_all | solution.py:161
  307.0 1.9 copy-start.1
  308.9 10.8 %copy-start = (bf16[40,64,128]{2,1,0:T(8,128)(2,1)}, bf16[40,64,128]{2,1,0:T(8,128)(2,1)S(1)}, u32[]{:S(2)}) copy-start(bf16[40,64,128]{2,1,0:T(8,128)(2,1)S(1)} %get-tuple-element.288) | copy-start | bytes 1966084 | tf_op jit(solution)/shard_map/while
  308.9 12.2 %copy-start.11 = (s32[11,32]{1,0:T(8,128)}, s32[11,32]{1,0:T(8,128)S(1)}, u32[]{:S(2)}) copy-start(s32[11,32]{1,0:T(8,128)S(1)} %get-tuple-element.287) | copy-start | bytes 4228 | tf_op jit(solution)/shard_map/while
  312.8 29.8 %all-to-all-start = ((bf16[32,64,256]{2,1,0:T(8,128)(2,1)}), bf16[32,64,256]{2,1,0:T(8,128)(2,1)S(1)}, u32[]{:S(2)}, u32[]{:S(2)}) async-start(bf16[32,64,256]{2,1,0:T(8,128)(2,1)} %select_select_fusion.3), calls=%async_computation | async-start | bytes 2097152 | tf_op jit(solution)/shard_map/while/body/eval_jaxpr/all_to_all | solution.py:161
  346.3 1.9 copy-start.1
  348.3 10.8 %copy-start = (bf16[40,64,128]{2,1,0:T(8,128)(2,1)}, bf16[40,64,128]{2,1,0:T(8,128)(2,1)S(1)}, u32[]{:S(2)}) copy-start(bf16[40,64,128]{2,1,0:T(8,128)(2,1)S(1)} %get-tuple-element.288) | copy-start | bytes 1966084 | tf_op jit(solution)/shard_map/while
  348.3 12.2 %copy-start.11 = (s32[11,32]{1,0:T(8,128)}, s32[11,32]{1,0:T(8,128)S(1)}, u32[]{:S(2)}) copy-start(s32[11,32]{1,0:T(8,128)S(1)} %get-tuple-element.287) | copy-start | bytes 4228 | tf_op jit(solution)/shard_map/while
  352.1 29.8 %all-to-all-start = ((bf16[32,64,256]{2,1,0:T(8,128)(2,1)}), bf16[32,64,256]{2,1,0:T(8,128)(2,1)S(1)}, u32[]{:S(2)}, u32[]{:S(2)}) async-start(bf16[32,64,256]{2,1,0:T(8,128)(2,1)} %select_select_fusion.3), calls=%async_computation | async-start | bytes 2097152 | tf_op jit(solution)/shard_map/while/body/eval_jaxpr/all_to_all | solution.py:161
  385.7 1.9 copy-start.1
  387.6 10.8 %copy-start = (bf16[40,64,128]{2,1,0:T(8,128)(2,1)}, bf16[40,64,128]{2,1,0:T(8,128)(2,1)S(1)}, u32[]{:S(2)}) copy-start(bf16[40,64,128]{2,1,0:T(8,128)(2,1)S(1)} %get-tuple-element.288) | copy-start | bytes 1966084 | tf_op jit(solution)/shard_map/while
  387.6 12.2 %copy-start.11 = (s32[11,32]{1,0:T(8,128)}, s32[11,32]{1,0:T(8,128)S(1)}, u32[]{:S(2)}) copy-start(s32[11,32]{1,0:T(8,128)S(1)} %get-tuple-element.287) | copy-start | bytes 4228 | tf_op jit(solution)/shard_map/while
  391.5 29.8 %all-to-all-start = ((bf16[32,64,256]{2,1,0:T(8,128)(2,1)}), bf16[32,64,256]{2,1,0:T(8,128)(2,1)S(1)}, u32[]{:S(2)}, u32[]{:S(2)}) async-start(bf16[32,64,256]{2,1,0:T(8,128)(2,1)} %select_select_fusion.3), calls=%async_computation | async-start | bytes 2097152 | tf_op jit(solution)/shard_map/while/body/eval_jaxpr/all_to_all | solution.py:161
  425.1 1.9 copy-start.1
  427.0 10.8 %copy-start = (bf16[40,64,128]{2,1,0:T(8,128)(2,1)}, bf16[40,64,128]{2,1,0:T(8,128)(2,1)S(1)}, u32[]{:S(2)}) copy-start(bf16[40,64,128]{2,1,0:T(8,128)(2,1)S(1)} %get-tuple-element.288) | copy-start | bytes 1966084 | tf_op jit(solution)/shard_map/while
  427.0 12.2 %copy-start.11 = (s32[11,32]{1,0:T(8,128)}, s32[11,32]{1,0:T(8,128)S(1)}, u32[]{:S(2)}) copy-start(s32[11,32]{1,0:T(8,128)S(1)} %get-tuple-element.287) | copy-start | bytes 4228 | tf_op jit(solution)/shard_map/while
  430.8 29.8 %all-to-all-start = ((bf16[32,64,256]{2,1,0:T(8,128)(2,1)}), bf16[32,64,256]{2,1,0:T(8,128)(2,1)S(1)}, u32[]{:S(2)}, u32[]{:S(2)}) async-start(bf16[32,64,256]{2,1,0:T(8,128)(2,1)} %select_select_fusion.3), calls=%async_computation | async-start | bytes 2097152 | tf_op jit(solution)/shard_map/while/body/eval_jaxpr/all_to_all | solution.py:161
  464.4 1.9 copy-start.1
  469.4 23.9 %copy-start.13 = (bf16[128,40]{0,1:T(8,128)(2,1)S(1)}, bf16[128,40]{0,1:T(8,128)(2,1)}, u32[]{:S(2)}) copy-start(bf16[128,40]{0,1:T(8,128)(2,1)} %param.11) | copy-start | bytes 30724
  469.4 24.0 %copy-start.7 = (bf16[128,2560]{1,0:T(8,128)(2,1)S(1)}, bf16[128,2560]{1,0:T(8,128)(2,1)}, u32[]{:S(2)}) copy-start(bf16[128,2560]{1,0:T(8,128)(2,1)} %param.10) | copy-start | bytes 1966084
  493.2 18.4 %copy-start.8 = (f32[128,20,128]{0,2,1:T(8,128)S(1)}, f32[128,20,128]{0,2,1:T(8,128)}, u32[]{:S(2)}) copy-start(f32[128,20,128]{0,2,1:T(8,128)} %copy.95) | copy-start | bytes 3932164
  (37 other events, 53.8 us)
where the time goes:
time: 516 us; the launch traced here: 513 us
  waiting for transfers between devices  235 us (46%)
  starting transfers between devices  76 us (15%)
  local copies, waits for them, and re-layouts  61.1 us (12%)
  matrix products  48.6 us (9%)
  other arithmetic  48.2 us (9%)
  blocking collectives  41.3 us (8%)
    all_to_all x11, waiting for transfers between devices, one_round(): lax.all_to_all(held_pairs(incoming), 'cubes', split_axis=0, concat_axis=0...  235 us
    all_to_all x11, starting transfers between devices, one_round(): lax.all_to_all(held_pairs(incoming), 'cubes', split_axis=0, concat_axis=0...  76 us
    all_gather x1, blocking collectives, body(): piece_keys = lax.all_gather(pooled_keys, 'cubes', axis=0, tiled=True)  23.3 us
    gather x3, other arithmetic, body(): jnp.take(position, selection.reshape(-1))  21.6 us
    gather x11, local copies, waits for them, and re-layouts, held_pairs(): picked = jnp.take(pair_groups, source, axis=0)  21.3 us
    dot_general x11, matrix products, merge_slots(): jnp.dot(onehot, weighted, precision=lax.Precision.HIGHEST)  20.3 us
    all_gather x1, blocking collectives, body(): piece_values = lax.all_gather(pooled_values, 'cubes', axis=0, tiled=True)  18 us
    dot_general x11, matrix products, block_partials(): jnp.einsum('sqd,skd->sqk', query_slots, slot_keys, preferred_element_type...  16.8 us
  transfers between devices with their start and end apart: 11, of which 11 were waited for; matrix products, arithmetic and copies ran while one was open for 3% of the time, Pallas kernels for 0%

commit v1 on v0

--- a/solution.py
+++ b/solution.py
@@ -1,11 +1,20 @@
+import functools
 import math
 
 import jax
 import jax.numpy as jnp
 from jax import lax
+from jax.experimental import pallas as pl
+from jax.experimental.pallas import tpu as pltpu
 from jax.sharding import PartitionSpec as P
 
 CUBE = 64
+HEADS_PER_CHUNK = 4
+LOOKAHEAD = 2
+
+
+def X_FIRST(chunk_count):
+    return (chunk_count // 2,)
 
 
 NEG_START = -1e30
@@ -57,7 +66,7 @@
     )
 
 
-def body(query_rows, key_rows, value_rows, gate_logits, selection, cube_ids):
+def streamed_body(query_rows, key_rows, value_rows, gate_logits, selection, cube_ids):
     device_count = lax.axis_size("cubes")
     token_count = query_rows.shape[0]
     feature_width = query_rows.shape[1]
@@ -182,6 +191,329 @@
     mixed = gates[:, :head_count, None] * coarse + gates[:, head_count:, None] * fine
     return mixed.reshape(token_count, feature_width).astype(jnp.bfloat16)
 
+CORES = 2
+TILE_ROWS = 16
+VMEM_BUDGET = 40 * 1024 * 1024
+
+
+def grid_of(device_count):
+    chips = device_count // CORES
+    x_extent = 1
+    for extent in range(1, chips + 1):
+        if chips % extent == 0 and extent**3 <= chips:
+            x_extent = extent
+    return (chips // x_extent, x_extent)
+
+
+def head_chunks(head_count):
+    chunk_heads = HEADS_PER_CHUNK if head_count % HEADS_PER_CHUNK == 0 else 1
+    chunk_count = head_count // chunk_heads
+    return (chunk_heads, chunk_count, set(X_FIRST(chunk_count)))
+
+
+def attention_kernel(
+    sizes, target_ref, query_ref, key_ref, value_ref, gate_ref, out_ref, *scratch
+):
+    device_count, head_count, head_size, local_cubes, picks = sizes
+    chunk_heads, chunk_count, x_first = head_chunks(head_count)
+    z_extent, x_extent = grid_of(device_count)
+    buffers = scratch[:chunk_count]
+    pool_ref = scratch[chunk_count]
+    send_sem, recv_sem = scratch[chunk_count + 1 :]
+    width = chunk_heads * head_size
+    token_count = query_ref.shape[0]
+    factor = 1.0 / math.sqrt(head_size)
+    z_stride = x_extent * CORES
+    me = lax.axis_index("cubes")
+    z = me // z_stride
+    x = (me // CORES) % x_extent
+    core = me % CORES
+    sibling = me + 1 - 2 * core
+    across = me + CORES * (1 - 2 * x)
+    has_up = z < z_extent - 1
+    has_down = z > 0
+    partners = {
+        "up": (me + z_stride, has_up),
+        "down": (me - z_stride, has_down),
+        "across": (across, None),
+        "sibling": (sibling, None),
+    }
+
+    def when(condition, action):
+        if condition is None:
+            action()
+        else:
+            pl.when(condition)(action)
+
+    def both(a, b):
+        if a is None:
+            return b
+        return a if b is None else jnp.logical_and(a, b)
+
+    def region(chunk, source):
+        if chunk == chunk_count:
+            return pool_ref.at[pl.ds(pl.multiple_of(source * TILE_ROWS, TILE_ROWS), TILE_ROWS), :]
+        return buffers[chunk].at[pl.ds(source * local_cubes, local_cubes)]
+
+    used = [0] * (chunk_count + 1)
+    sent = []
+
+    def forward(chunk, source, condition, ways):
+        for way in ways:
+            partner, exists = partners[way]
+            slot = used[chunk]
+            used[chunk] += 1
+            holds = both(condition, exists)
+            copy = functools.partial(
+                pltpu.make_async_remote_copy,
+                send_sem=send_sem.at[chunk, slot],
+                recv_sem=recv_sem.at[chunk, source],
+                device_id={"cubes": partner},
+                device_id_type=pl.DeviceIdType.MESH,
+            )
+
+            def start(copy=copy):
+                copy(region(chunk, source), region(chunk, source)).start()
+
+            def finish(copy=copy):
+                copy(region(chunk, source), region(chunk, source)).wait_send()
+
+            when(holds, start)
+            sent.append((holds, finish))
+
+    def arrive(chunk, source, condition):
+        def take():
+            pltpu.make_async_remote_copy(
+                src_ref=region(chunk, source),
+                dst_ref=region(chunk, source),
+                send_sem=send_sem.at[chunk, 0],
+                recv_sem=recv_sem.at[chunk, source],
+                device_id={"cubes": sibling},
+                device_id_type=pl.DeviceIdType.MESH,
+            ).wait_recv()
+
+        when(condition, take)
+
+    def fill(chunk):
+        columns = slice(chunk * width, (chunk + 1) * width)
+        for cube in range(local_cubes):
+            rows = slice(cube * CUBE, (cube + 1) * CUBE)
+            buffers[chunk][me * local_cubes + cube, 0] = key_ref[rows, columns]
+            buffers[chunk][me * local_cubes + cube, 1] = value_ref[rows, columns]
+
+    parts = TILE_ROWS // (2 * local_cubes)
+    part_heads = head_count // parts
+    part_width = part_heads * head_size
+
+    def fill_pool():
+        rows = []
+        for part in range(parts):
+            columns = slice(part * part_width, (part + 1) * part_width)
+            for ref in (key_ref, value_ref):
+                for cube in range(local_cubes):
+                    block = ref[cube * CUBE : (cube + 1) * CUBE, columns].astype(jnp.float32)
+                    rows.append(jnp.sum(block, axis=0, keepdims=True) * (1.0 / CUBE))
+        pool_ref[pl.ds(pl.multiple_of(me * TILE_ROWS, TILE_ROWS), TILE_ROWS), :] = jnp.concatenate(
+            rows, axis=0
+        ).astype(jnp.bfloat16)
+
+    def compute(chunk):
+        buffer = buffers[chunk]
+
+        def one_head(inner, carry):
+            head = chunk * chunk_heads + inner
+            columns = pl.ds(pl.multiple_of(inner * head_size, head_size), head_size)
+            head_columns = pl.ds(pl.multiple_of(head * head_size, head_size), head_size)
+            part = head // part_heads
+            pool_columns = pl.ds(
+                pl.multiple_of((head % part_heads) * head_size, head_size), head_size
+            )
+            queries = query_ref[:, head_columns]
+            pooled = pool_ref[:, pool_columns]
+            scores = (
+                lax.dot_general(
+                    queries, pooled, (((1,), (1,)), ((), ())), preferred_element_type=jnp.float32
+                )
+                * factor
+            )
+            row = lax.broadcasted_iota(jnp.int32, scores.shape, 1) & (TILE_ROWS - 1)
+            first = part * (2 * local_cubes)
+            valid = (row >= first) & (row < first + local_cubes)
+            scores = jnp.where(valid, scores, -jnp.inf)
+            weights = jnp.exp(scores - jnp.max(scores, axis=1, keepdims=True))
+            total = jnp.sum(weights, axis=1, keepdims=True)
+            moved = pltpu.roll(weights, local_cubes, 1).astype(jnp.bfloat16)
+            coarse = jnp.dot(moved, pooled, preferred_element_type=jnp.float32) / total
+            gates = gate_ref[...].astype(jnp.float32)
+            lane = lax.broadcasted_iota(jnp.int32, gates.shape, 1)
+            coarse_gate = jax.nn.sigmoid(
+                jnp.sum(jnp.where(lane == head, gates, 0.0), axis=1, keepdims=True)
+            )
+            fine_gate = jax.nn.sigmoid(
+                jnp.sum(jnp.where(lane == head + head_count, gates, 0.0), axis=1, keepdims=True)
+            )
+            fine = []
+            for cube in range(local_cubes):
+                base = (cube * head_count + head) * picks
+                chosen = [target_ref[base + pick] for pick in range(picks)]
+                keys = jnp.concatenate([buffer[t, 0, :, columns] for t in chosen], axis=0)
+                values = jnp.concatenate([buffer[t, 1, :, columns] for t in chosen], axis=0)
+                scores = (
+                    lax.dot_general(
+                        queries[cube * CUBE : (cube + 1) * CUBE],
+                        keys,
+                        (((1,), (1,)), ((), ())),
+                        preferred_element_type=jnp.float32,
+                    )
+                    * factor
+                )
+                weights = jnp.exp(scores - jnp.max(scores, axis=1, keepdims=True))
+                total = jnp.sum(weights, axis=1, keepdims=True)
+                fine.append(
+                    jnp.dot(
+                        weights.astype(jnp.bfloat16), values, preferred_element_type=jnp.float32
+                    )
+                    / total
+                )
+            fine = jnp.concatenate(fine, axis=0)
+            out_ref[:, head_columns] = (coarse_gate * coarse + fine_gate * fine).astype(
+                out_ref.dtype
+            )
+            return carry
+
+        lax.fori_loop(0, chunk_heads, one_head, 0)
+
+    events = []
+    hop = 0.7
+
+    def add(key, action):
+        events.append((key, len(events), action))
+
+    def own(chunk):
+        if chunk < chunk_count:
+            fill(chunk)
+        forward(chunk, me, None, ("up", "down", "across", "sibling"))
+
+    def passing(chunk, source, condition, ways):
+        arrive(chunk, source, condition)
+        forward(chunk, source, condition, ways)
+
+    def plan(chunk, time, crosses_first):
+        add(time - LOOKAHEAD, lambda: own(chunk))
+        other = me + CORES * (1 - 2 * x)
+        if crosses_first:
+            add(time - 0.5, lambda: passing(chunk, other, None, ("up", "down", "sibling")))
+        else:
+            add(time + 0.1, lambda: passing(chunk, other, None, ("sibling",)))
+        for distance in range(1, z_extent):
+            for way, source_step, condition in (
+                ("up", -distance, z >= distance),
+                ("down", distance, z < z_extent - distance),
+            ):
+                near = me + source_step * z_stride
+                far = other + source_step * z_stride
+                key = time + hop * (distance - 1)
+                if crosses_first:
+                    add(key, functools.partial(passing, chunk, near, condition, (way, "sibling")))
+                    add(
+                        key + 0.3,
+                        functools.partial(passing, chunk, far, condition, (way, "sibling")),
+                    )
+                else:
+                    add(
+                        key,
+                        functools.partial(passing, chunk, near, condition, (way, "across", "sibling")),
+                    )
+                    add(
+                        key + 1.0, functools.partial(passing, chunk, far, condition, ("sibling",))
+                    )
+
+        def complete():
+            for place in range(z_extent * x_extent):
+                arrive(chunk, place * CORES + (1 - core), None)
+            if chunk < chunk_count:
+                compute(chunk)
+
+        add(time + (z_extent - 2) * hop + 1.1, complete)
+
+    plan(chunk_count, -1.0, False)
+    for chunk in range(chunk_count):
+        plan(chunk, float(chunk), chunk in x_first)
+
+    barrier = pltpu.get_barrier_semaphore()
+    for partner, exists in partners.values():
+
+        def greet(partner=partner):
+            pl.semaphore_signal(
+                barrier, inc=1, device_id={"cubes": partner}, device_id_type=pl.DeviceIdType.MESH
+            )
+
+        when(exists, greet)
+    fill_pool()
+    pl.semaphore_wait(barrier, 2 + has_up.astype(jnp.int32) + has_down.astype(jnp.int32))
+    for key, order, action in sorted(events, key=lambda event: event[:2]):
+        action()
+    for holds, finish in sent:
+        when(holds, finish)
+
+
+def gathered_body(query_rows, key_rows, value_rows, gate_logits, selection, cube_ids):
+    device_count = lax.axis_size("cubes")
+    token_count, feature_width = query_rows.shape
+    head_count = gate_logits.shape[1] // 2
+    head_size = feature_width // head_count
+    local_cubes = token_count // CUBE
+    total_cubes = cube_ids.shape[0]
+    picks = selection.shape[2]
+    self_index = lax.axis_index("cubes")
+    chosen = lax.dynamic_slice_in_dim(selection, self_index * local_cubes, local_cubes, 0)
+    cube_range = jnp.arange(total_cubes, dtype=jnp.int32)
+    targets = jnp.sum(
+        jnp.where(chosen.reshape(-1)[:, None] == cube_ids[None, :], cube_range[None, :], 0), axis=1
+    )
+    chunk_heads, chunk_count, unused = head_chunks(head_count)
+    width = chunk_heads * head_size
+    z_extent, x_extent = grid_of(device_count)
+    sends = 4 + 3 * 4 * (z_extent - 1) + 3
+    pool_width = head_count * head_size * 2 * local_cubes // TILE_ROWS
+    sizes = (device_count, head_count, head_size, local_cubes, picks)
+    return pl.pallas_call(
+        functools.partial(attention_kernel, sizes),
+        out_shape=jax.ShapeDtypeStruct((token_count, feature_width), jnp.bfloat16),
+        in_specs=[pl.BlockSpec(memory_space=pltpu.SMEM)]
+        + [pl.BlockSpec(memory_space=pltpu.VMEM)] * 4,
+        out_specs=pl.BlockSpec(memory_space=pltpu.VMEM),
+        scratch_shapes=[
+            pltpu.VMEM((total_cubes, 2, CUBE, width), jnp.bfloat16) for unused in range(chunk_count)
+        ]
+        + [
+            pltpu.VMEM((device_count * TILE_ROWS, pool_width), jnp.bfloat16),
+            pltpu.SemaphoreType.DMA((chunk_count + 1, sends)),
+            pltpu.SemaphoreType.DMA((chunk_count + 1, device_count)),
+        ],
+        compiler_params=pltpu.CompilerParams(
+            collective_id=0, has_side_effects=True, vmem_limit_bytes=VMEM_BUDGET
+        ),
+    )(targets, query_rows, key_rows, value_rows, gate_logits)
+
+
+def body(query_rows, key_rows, value_rows, gate_logits, selection, cube_ids):
+    device_count = lax.axis_size("cubes")
+    token_count, feature_width = query_rows.shape
+    head_count = gate_logits.shape[1] // 2
+    local_cubes = token_count // CUBE
+    gathered_bytes = 2 * device_count * token_count * feature_width * key_rows.dtype.itemsize
+    fits = (
+        2 * gathered_bytes // 3 <= VMEM_BUDGET // 2
+        and device_count % CORES == 0
+        and grid_of(device_count)[1] == 2
+        and TILE_ROWS % (2 * local_cubes) == 0
+        and head_count % (TILE_ROWS // (2 * local_cubes)) == 0
+    )
+    return (gathered_body if fits else streamed_body)(
+        query_rows, key_rows, value_rows, gate_logits, selection, cube_ids
+    )
+
 
 def solution(mesh):
     placed = (

time: 516 us -> 135 us (0.26)
  waiting for transfers between devices: 235 us -> 0 us
  Pallas kernels: 0 us -> 128 us
  starting transfers between devices: 76 us -> 0 us
  local copies, waits for them, and re-layouts: 61.1 us -> 5.95 us
  matrix products: 48.6 us -> 0 us
  other arithmetic: 48.2 us -> 0.09 us
  blocking collectives: 41.3 us -> 0 us
    all_to_all x11 -> x0, waiting for transfers between devices: 235 us -> none  [one_round(): lax.all_to_all(held_pairs(incoming), 'cubes', split_axis=0, concat_axis=0...]
    pallas_call x0 -> x1, Pallas kernels: none -> 128 us  [gathered_body(): pl.pallas_call(functools.partial(attention_kernel, sizes), out_shape=jax....]
    all_to_all x11 -> x0, starting transfers between devices: 76 us -> none  [one_round(): lax.all_to_all(held_pairs(incoming), 'cubes', split_axis=0, concat_axis=0...]
    dot_general x46 -> x0, matrix products: 48.6 us -> none  [the longest x11 20.3 us: merge_slots(): jnp.dot(onehot, weighted, precision=lax.Precision.HIGHEST)]
    gather x36 -> x0, local copies, waits for them, and re-layouts: 44.7 us -> none  [the longest x11 21.3 us: held_pairs(): picked = jnp.take(pair_groups, source, axis=0)]
    all_gather x2 -> x0, blocking collectives: 41.3 us -> none  [the longest x1 23.3 us: body(): piece_keys = lax.all_gather(pooled_keys, 'cubes', axis=0, tiled=True)]
    gather x25 -> x0, other arithmetic: 21.8 us -> none  [the longest x3 21.6 us: body(): jnp.take(position, selection.reshape(-1))]
    select_n x23 -> x0, other arithmetic: 13.3 us -> none  [the longest x11 13.2 us: held_pairs(): jnp.where((incoming >= 0).reshape(-1)[:, None, None], picked, jnp.zeros((...]
  transfers between devices with their start and end apart: 11 -> 0, of which waited for: 11 -> 0; matrix products, arithmetic and copies ran while one was open for 3% -> 0% of each run, Pallas kernels for 0% -> 0%
where the time goes in v1:
time: 135 us; the launch traced here: 134 us
  Pallas kernels  128 us (95%)
  local copies, waits for them, and re-layouts  5.95 us (4%)
    pallas_call x1, Pallas kernels, gathered_body(): pl.pallas_call(functools.partial(attention_kernel, sizes), out_shape=jax....  128 us
    unnamed x14, local copies, waits for them, and re-layouts  5.56 us

profile of v1, /device:TPU:0, one launch (start us, length us, event | category | flops | bytes accessed | tf_op | source)
XLA Modules:
  0.0 133.9 jit_solution(1718254447581777606)
XLA Ops:
  0.0 0.0 copy-start
  0.0 0.0 copy-start.4
  0.0 0.7 copy-done.4
  0.7 0.1 copy.11.gate_ref
  0.9 0.0 copy-done
  0.9 0.1 constant_dynamic-slice_fusion
  1.0 0.2 copy.10
  1.2 0.0 copy-start.5
  1.2 0.1 eq.15
  1.3 0.6 copy-done.5
  1.9 0.1 select_reduce_fusion.target_ref
  2.0 0.0 copy-start.1
  2.0 1.1 copy-done.1
  3.0 0.0 copy-start.2
  3.0 1.1 copy-done.2
  4.1 0.0 copy-start.3
  4.1 1.1 copy-done.3
  5.2 127.8 %shard_map.64 = bf16[128,2560]{1,0:T(8,128)(2,1)S(1)} custom-call(s32[320]{0:T(512)S(1)} %select_reduce_fusion.target_ref, bf16[128,2560]{1,0:T(8,128)(2,1)S(1)} %copy-done.1, bf16[128,2560]{1,0:T(8,128)(2,1)S(1)} %copy-done.2, bf16[128,2560]{1,0:T(8,128)(2,1)S(1)} %copy-done.3, bf16[128,40]{1,0:T(8,128)(2,1)S(1)} %copy.11.gate_ref), custom_call_target="tpu_custom_call" | custom-call | tf_op jit(solution)/shard_map/pallas_call | solution.py:480
  133.0 0.8 copy.13
Async XLA Ops:
  0.0 0.9 copy-start
  0.0 0.7 copy-start.4
  1.2 0.7 copy-start.5
  2.0 1.1 copy-start.1
  3.0 1.1 copy-start.2
  4.1 1.1 copy-start.3

commit v2 on v1

--- a/solution.py
+++ b/solution.py
@@ -9,12 +9,13 @@
 from jax.sharding import PartitionSpec as P
 
 CUBE = 64
-HEADS_PER_CHUNK = 4
-LOOKAHEAD = 2
+HEADS_PER_CHUNK = 2
+LOOKAHEAD = 3
+SLACK = 0.5
 
 
 def X_FIRST(chunk_count):
-    return (chunk_count // 2,)
+    return (chunk_count // 2 - 1, chunk_count - 1)
 
 
 NEG_START = -1e30
@@ -194,6 +195,7 @@
 CORES = 2
 TILE_ROWS = 16
 VMEM_BUDGET = 40 * 1024 * 1024
+VMEM_GRANT = 62 * 1024 * 1024
 
 
 def grid_of(device_count):
@@ -212,16 +214,15 @@
 
 
 def attention_kernel(
-    sizes, target_ref, query_ref, key_ref, value_ref, gate_ref, out_ref, *scratch
+    sizes, target_ref, query_rows, key_cubes, value_cubes, gate_rows, out_ref, *scratch
 ):
     device_count, head_count, head_size, local_cubes, picks = sizes
     chunk_heads, chunk_count, x_first = head_chunks(head_count)
     z_extent, x_extent = grid_of(device_count)
     buffers = scratch[:chunk_count]
     pool_ref = scratch[chunk_count]
-    send_sem, recv_sem = scratch[chunk_count + 1 :]
+    query_ref, gate_ref, send_sem, recv_sem, local_sem = scratch[chunk_count + 1 :]
     width = chunk_heads * head_size
-    token_count = query_ref.shape[0]
     factor = 1.0 / math.sqrt(head_size)
     z_stride = x_extent * CORES
     me = lax.axis_index("cubes")
@@ -255,14 +256,14 @@
             return pool_ref.at[pl.ds(pl.multiple_of(source * TILE_ROWS, TILE_ROWS), TILE_ROWS), :]
         return buffers[chunk].at[pl.ds(source * local_cubes, local_cubes)]
 
-    used = [0] * (chunk_count + 1)
+    slots = {}
     sent = []
 
-    def forward(chunk, source, condition, ways):
+    def forward(chunk, source, condition, ways, name):
         for way in ways:
             partner, exists = partners[way]
-            slot = used[chunk]
-            used[chunk] += 1
+            turn = "z" if way in ("up", "down") and name[0] in ("near", "far") else way
+            slot = slots.setdefault((chunk, name, turn), sum(key[0] == chunk for key in slots))
             holds = both(condition, exists)
             copy = functools.partial(
                 pltpu.make_async_remote_copy,
@@ -294,33 +295,48 @@
 
         when(condition, take)
 
-    def fill(chunk):
-        columns = slice(chunk * width, (chunk + 1) * width)
-        for cube in range(local_cubes):
-            rows = slice(cube * CUBE, (cube + 1) * CUBE)
-            buffers[chunk][me * local_cubes + cube, 0] = key_ref[rows, columns]
-            buffers[chunk][me * local_cubes + cube, 1] = value_ref[rows, columns]
+    def fills(chunk):
+        columns = pl.ds(chunk * width, width)
+        mine = pl.ds(me * local_cubes, local_cubes)
+        return [
+            pltpu.make_async_copy(
+                ref.at[:, :, columns], buffers[chunk].at[mine, kind], local_sem.at[chunk, kind]
+            )
+            for kind, ref in enumerate((key_cubes, value_cubes))
+        ]
+
+    def query_fills():
+        return [
+            pltpu.make_async_copy(query_rows, query_ref, local_sem.at[chunk_count, 0]),
+            pltpu.make_async_copy(gate_rows, gate_ref, local_sem.at[chunk_count, 1]),
+        ]
 
     parts = TILE_ROWS // (2 * local_cubes)
     part_heads = head_count // parts
-    part_width = part_heads * head_size
 
     def fill_pool():
+        def mean_row(head, kind, cube):
+            start = (head % chunk_heads) * head_size
+            buffer = buffers[head // chunk_heads]
+            block = buffer[me * local_cubes + cube, kind, :, start : start + head_size]
+            return jnp.sum(block.astype(jnp.float32), axis=0, keepdims=True) * (1.0 / CUBE)
+
         rows = []
         for part in range(parts):
-            columns = slice(part * part_width, (part + 1) * part_width)
-            for ref in (key_ref, value_ref):
+            heads = range(part * part_heads, (part + 1) * part_heads)
+            for kind in range(2):
                 for cube in range(local_cubes):
-                    block = ref[cube * CUBE : (cube + 1) * CUBE, columns].astype(jnp.float32)
-                    rows.append(jnp.sum(block, axis=0, keepdims=True) * (1.0 / CUBE))
+                    rows.append(
+                        jnp.concatenate([mean_row(head, kind, cube) for head in heads], axis=1)
+                    )
         pool_ref[pl.ds(pl.multiple_of(me * TILE_ROWS, TILE_ROWS), TILE_ROWS), :] = jnp.concatenate(
             rows, axis=0
         ).astype(jnp.bfloat16)
 
-    def compute(chunk):
+    def compute(chunk, inner):
         buffer = buffers[chunk]
 
-        def one_head(inner, carry):
+        def one_head():
             head = chunk * chunk_heads + inner
             columns = pl.ds(pl.multiple_of(inner * head_size, head_size), head_size)
             head_columns = pl.ds(pl.multiple_of(head * head_size, head_size), head_size)
@@ -379,9 +395,8 @@
             out_ref[:, head_columns] = (coarse_gate * coarse + fine_gate * fine).astype(
                 out_ref.dtype
             )
-            return carry
-
-        lax.fori_loop(0, chunk_heads, one_head, 0)
+
+        one_head()
 
     events = []
     hop = 0.7
@@ -389,22 +404,29 @@
     def add(key, action):
         events.append((key, len(events), action))
 
+    filled = set()
+
     def own(chunk):
-        if chunk < chunk_count:
-            fill(chunk)
-        forward(chunk, me, None, ("up", "down", "across", "sibling"))
-
-    def passing(chunk, source, condition, ways):
+        for needed in range(chunk_count) if chunk == chunk_count else (chunk,):
+            if needed not in filled:
+                filled.add(needed)
+                for copy in fills(needed):
+                    copy.wait()
+        if chunk == chunk_count:
+            fill_pool()
+        forward(chunk, me, None, ("up", "down", "across", "sibling"), ("own", 0))
+
+    def passing(chunk, source, condition, ways, name):
         arrive(chunk, source, condition)
-        forward(chunk, source, condition, ways)
-
-    def plan(chunk, time, crosses_first):
-        add(time - LOOKAHEAD, lambda: own(chunk))
+        forward(chunk, source, condition, ways, name)
+
+    def plan(chunk, time, crosses_first, own_time):
+        add(own_time, lambda: own(chunk))
         other = me + CORES * (1 - 2 * x)
         if crosses_first:
-            add(time - 0.5, lambda: passing(chunk, other, None, ("up", "down", "sibling")))
+            add(time - 0.5, lambda: passing(chunk, other, None, ("up", "down", "sibling"), ("other", 0)))
         else:
-            add(time + 0.1, lambda: passing(chunk, other, None, ("sibling",)))
+            add(time + 0.1, lambda: passing(chunk, other, None, ("sibling",), ("other", 0)))
         for distance in range(1, z_extent):
             for way, source_step, condition in (
                 ("up", -distance, z >= distance),
@@ -413,33 +435,37 @@
                 near = me + source_step * z_stride
                 far = other + source_step * z_stride
                 key = time + hop * (distance - 1)
-                if crosses_first:
-                    add(key, functools.partial(passing, chunk, near, condition, (way, "sibling")))
-                    add(
-                        key + 0.3,
-                        functools.partial(passing, chunk, far, condition, (way, "sibling")),
-                    )
-                else:
-                    add(
-                        key,
-                        functools.partial(passing, chunk, near, condition, (way, "across", "sibling")),
-                    )
-                    add(
-                        key + 1.0, functools.partial(passing, chunk, far, condition, ("sibling",))
-                    )
+                turn = distance if way == "up" else z_extent - distance
+                onward = (way, "sibling") if crosses_first else (way, "across", "sibling")
+                far_onward = (way, "sibling") if crosses_first else ("sibling",)
+                far_key = key + (0.3 if crosses_first else 1.0)
+                for moment, source, ways, name in (
+                    (key, near, onward, ("near", turn)),
+                    (far_key, far, far_onward, ("far", turn)),
+                ):
+                    add(moment, functools.partial(passing, chunk, source, condition, ways, name))
 
         def complete():
             for place in range(z_extent * x_extent):
                 arrive(chunk, place * CORES + (1 - core), None)
-            if chunk < chunk_count:
-                compute(chunk)
-
-        add(time + (z_extent - 2) * hop + 1.1, complete)
-
-    plan(chunk_count, -1.0, False)
+
+        end = time + (z_extent - 2) * hop + 1.1
+        if chunk == chunk_count:
+            add(end, complete)
+            return
+        add(end + SLACK, complete)
+        for inner in range(chunk_heads):
+            add(end + SLACK + inner / chunk_heads, functools.partial(compute, chunk, inner))
+
+    plan(chunk_count, 0.3, False, -0.9)
     for chunk in range(chunk_count):
-        plan(chunk, float(chunk), chunk in x_first)
-
+        plan(chunk, float(chunk), chunk in x_first, float(chunk - LOOKAHEAD))
+
+    for chunk in range(chunk_count):
+        for copy in fills(chunk):
+            copy.start()
+    for copy in query_fills():
+        copy.start()
     barrier = pltpu.get_barrier_semaphore()
     for partner, exists in partners.values():
 
@@ -449,8 +475,9 @@
             )
 
         when(exists, greet)
-    fill_pool()
     pl.semaphore_wait(barrier, 2 + has_up.astype(jnp.int32) + has_down.astype(jnp.int32))
+    for copy in query_fills():
+        copy.wait()
     for key, order, action in sorted(events, key=lambda event: event[:2]):
         action()
     for holds, finish in sent:
@@ -474,27 +501,36 @@
     chunk_heads, chunk_count, unused = head_chunks(head_count)
     width = chunk_heads * head_size
     z_extent, x_extent = grid_of(device_count)
-    sends = 4 + 3 * 4 * (z_extent - 1) + 3
+    sends = 4 + 3 + 4 * (z_extent - 1)
     pool_width = head_count * head_size * 2 * local_cubes // TILE_ROWS
     sizes = (device_count, head_count, head_size, local_cubes, picks)
     return pl.pallas_call(
         functools.partial(attention_kernel, sizes),
         out_shape=jax.ShapeDtypeStruct((token_count, feature_width), jnp.bfloat16),
         in_specs=[pl.BlockSpec(memory_space=pltpu.SMEM)]
-        + [pl.BlockSpec(memory_space=pltpu.VMEM)] * 4,
+        + [pl.BlockSpec(memory_space=pltpu.HBM)] * 4,
         out_specs=pl.BlockSpec(memory_space=pltpu.VMEM),
         scratch_shapes=[
             pltpu.VMEM((total_cubes, 2, CUBE, width), jnp.bfloat16) for unused in range(chunk_count)
         ]
         + [
             pltpu.VMEM((device_count * TILE_ROWS, pool_width), jnp.bfloat16),
+            pltpu.VMEM(query_rows.shape, query_rows.dtype),
+            pltpu.VMEM(gate_logits.shape, gate_logits.dtype),
             pltpu.SemaphoreType.DMA((chunk_count + 1, sends)),
             pltpu.SemaphoreType.DMA((chunk_count + 1, device_count)),
+            pltpu.SemaphoreType.DMA((chunk_count + 1, 2)),
         ],
         compiler_params=pltpu.CompilerParams(
-            collective_id=0, has_side_effects=True, vmem_limit_bytes=VMEM_BUDGET
+            collective_id=0, has_side_effects=True, vmem_limit_bytes=VMEM_GRANT
         ),
-    )(targets, query_rows, key_rows, value_rows, gate_logits)
+    )(
+        targets,
+        query_rows,
+        key_rows.reshape(local_cubes, CUBE, feature_width),
+        value_rows.reshape(local_cubes, CUBE, feature_width),
+        gate_logits,
+    )
 
 
 def body(query_rows, key_rows, value_rows, gate_logits, selection, cube_ids):

time: 135 us -> 129 us (0.956)
  Pallas kernels: 128 us -> 123 us
  local copies, waits for them, and re-layouts: 5.95 us -> 4.38 us
    pallas_call x1, Pallas kernels: 128 us -> 123 us  [gathered_body(): pl.pallas_call(functools.partial(attention_kernel, sizes), out_shape=jax....]
    unnamed x14 -> x8, local copies, waits for them, and re-layouts: 5.56 us -> 4 us
where the time goes in v2:
time: 129 us
  Pallas kernels  123 us (95%)
  local copies, waits for them, and re-layouts  4.38 us (3%)
    pallas_call x1, Pallas kernels, gathered_body(): pl.pallas_call(functools.partial(attention_kernel, sizes), out_shape=jax....  123 us
    unnamed x8, local copies, waits for them, and re-layouts  4 us

profile of v2, /device:TPU:0, one launch (start us, length us, event | category | flops | bytes accessed | tf_op | source)
XLA Modules:
  0.0 128.5 jit_solution(1545029233359400264)
XLA Ops:
  0.0 0.0 copy-start
  0.0 0.0 copy-start.1
  0.0 0.7 copy-done.1
  0.7 0.7 copy.11.gate_rows
  1.5 0.0 copy-done
  1.5 0.1 constant_dynamic-slice_fusion
  1.6 0.2 copy.10
  1.8 0.0 copy-start.2
  1.8 0.1 eq.15
  1.9 0.6 copy-done.2
  2.4 0.7 select_reduce_fusion.target_ref
  3.1 123.5 %shard_map.64 = bf16[128,2560]{1,0:T(8,128)(2,1)} custom-call(s32[320]{0:T(512)} %select_reduce_fusion.target_ref, bf16[128,2560]{1,0:T(8,128)(2,1)} %query_rows.1, bf16[2,64,2560]{2,1,0:T(8,128)(2,1)} %bitcast.2, bf16[2,64,2560]{2,1,0:T(8,128)(2,1)} %bitcast.3, bf16[128,40]{1,0:T(8,128)(2,1)} %copy.11.gate_rows), custom_call_target="tpu_custom_call" | custom-call | tf_op jit(solution)/shard_map/pallas_call | solution.py:507
  126.6 2.0 %copy.13 = bf16[128,2560]{1,0:T(8,128)(2,1)} copy(bf16[128,2560]{1,0:T(8,128)(2,1)} %shard_map.64) | data formatting | bytes 1310720
Async XLA Ops:
  0.0 1.5 %copy-start = (s32[32,20,8]{0,2,1:T(8,128)S(1)}, s32[32,20,8]{0,2,1:T(8,128)}, u32[]{:S(2)}) copy-start(s32[32,20,8]{0,2,1:T(8,128)} %param.10) | copy-start | bytes 61444
  0.0 0.7 copy-start.1
  1.8 0.7 copy-start.2

commit v3 on v0

--- a/solution.py
+++ b/solution.py
@@ -1,11 +1,15 @@
+import functools
 import math
 
 import jax
 import jax.numpy as jnp
 from jax import lax
+from jax.experimental import pallas as pl
+from jax.experimental.pallas import tpu as pltpu
 from jax.sharding import PartitionSpec as P
 
 CUBE = 64
+LOOKAHEAD = 2
 
 
 NEG_START = -1e30
@@ -57,7 +61,7 @@
     )
 
 
-def body(query_rows, key_rows, value_rows, gate_logits, selection, cube_ids):
+def streamed_body(query_rows, key_rows, value_rows, gate_logits, selection, cube_ids):
     device_count = lax.axis_size("cubes")
     token_count = query_rows.shape[0]
     feature_width = query_rows.shape[1]
@@ -182,6 +186,338 @@
     mixed = gates[:, :head_count, None] * coarse + gates[:, head_count:, None] * fine
     return mixed.reshape(token_count, feature_width).astype(jnp.bfloat16)
 
+CORES = 2
+HALVES = 2
+SITES = 4
+VMEM_GRANT = 62 * 1024 * 1024
+
+
+def grid_of(device_count):
+    chips = device_count // CORES
+    x_extent = 1
+    for extent in range(1, chips + 1):
+        if chips % extent == 0 and extent**3 <= chips:
+            x_extent = extent
+    return (chips // x_extent, x_extent)
+
+
+def attention_kernel(
+    sizes,
+    position_ref,
+    selection_ref,
+    query_rows,
+    key_cubes,
+    value_cubes,
+    gate_rows,
+    out_ref,
+    *scratch,
+):
+    head_count, head_size, local_cubes, picks = sizes
+    site_heads = head_count // SITES
+    buffers = scratch[:site_heads]
+    (stage, query_ref, gate_ref, done, out_block) = scratch[site_heads : site_heads + 5]
+    (kv_send, kv_recv, query_send, query_recv, out_send, out_recv, kv_local, query_local) = scratch[
+        site_heads + 5 :
+    ]
+    factor = 1.0 / math.sqrt(head_size)
+    width = site_heads * head_size
+    me = lax.axis_index("cubes")
+    core = me % CORES
+    x = (me // CORES) % 2
+    low = (me // (2 * CORES)) % 2
+    half = me // (4 * CORES)
+    sibling = me + 1 - 2 * core
+
+    def flip(bit, on):
+        return bit + on * (1 - 2 * bit)
+
+    def device(turn):
+        return (
+            (flip(half, turn // 4) * 2 + flip(low, (turn // 2) % 2)) * 2 + flip(x, turn % 2)
+        ) * CORES + core
+
+    def group(turn):
+        return flip(x, turn % 2) * 2 + flip(low, (turn // 2) % 2)
+
+    def head_columns(head, count):
+        return pl.ds(pl.multiple_of(head * head_size, head_size), count * head_size)
+
+    def cubes_of(source):
+        return pl.ds(source * local_cubes, local_cubes)
+
+    def remote(source, target, send, recv, partner):
+        return pltpu.make_async_remote_copy(
+            src_ref=source,
+            dst_ref=target,
+            send_sem=send,
+            recv_sem=recv,
+            device_id={"cubes": partner},
+            device_id_type=pl.DeviceIdType.MESH,
+        )
+
+    def held(turn, inner):
+        if turn % SITES == 0:
+            return buffers[inner].at[cubes_of(me)]
+        return stage.at[turn % SITES - 1, inner]
+
+    def fills(turn, inner):
+        columns = head_columns(group(turn) * site_heads + inner, 1)
+        return [
+            pltpu.make_async_copy(
+                ref.at[:, :, columns], held(turn, inner).at[:, kind], kv_local.at[turn, inner, kind]
+            )
+            for kind, ref in enumerate((key_cubes, value_cubes))
+        ]
+
+    def own_queries():
+        columns = head_columns(group(0) * site_heads, site_heads)
+        return [
+            pltpu.make_async_copy(query_rows.at[:, columns], query_ref.at[0], query_local.at[0]),
+            pltpu.make_async_copy(gate_rows, gate_ref.at[0], query_local.at[1]),
+        ]
+
+    def query_copies(turn):
+        columns = head_columns(group(turn) * site_heads, site_heads)
+        return [
+            remote(
+                query_rows.at[:, columns],
+                query_ref.at[turn],
+                query_send.at[0, turn],
+                query_recv.at[0, turn],
+                device(turn),
+            ),
+            remote(
+                gate_ref.at[0],
+                gate_ref.at[turn],
+                query_send.at[1, turn],
+                query_recv.at[1, turn],
+                device(turn),
+            ),
+        ]
+
+    def kv_copy(turn, inner):
+        return remote(
+            held(turn, inner),
+            buffers[inner].at[cubes_of(me)],
+            kv_send.at[inner, turn],
+            kv_recv.at[inner, turn],
+            device(turn),
+        )
+
+    def kv_arrival(turn, inner):
+        region = buffers[inner].at[cubes_of(device(turn))]
+        return remote(
+            region, region, kv_send.at[inner, turn], kv_recv.at[inner, turn], device(turn)
+        )
+
+    turns = SITES * HALVES
+
+    def pass_on(turn, inner):
+        region = buffers[inner].at[cubes_of(device(turn))]
+        slot = turns + turn
+        return remote(region, region, kv_send.at[inner, slot], kv_recv.at[inner, slot], sibling)
+
+    def passed_arrival(turn, inner):
+        region = buffers[inner].at[cubes_of(device(turn) + 1 - 2 * core)]
+        slot = turns + turn
+        return remote(region, region, kv_send.at[inner, slot], kv_recv.at[inner, slot], sibling)
+
+    def out_copy(turn, inner):
+        columns = head_columns(group(0) * site_heads + inner, 1)
+        return remote(
+            done.at[inner, turn],
+            out_block.at[:, columns],
+            out_send.at[inner, turn],
+            out_recv.at[inner, turn],
+            device(turn),
+        )
+
+    def out_arrival(turn, inner):
+        columns = head_columns(group(turn) * site_heads + inner, 1)
+        return remote(
+            done.at[inner, turn],
+            out_block.at[:, columns],
+            out_send.at[inner, turn],
+            out_recv.at[inner, turn],
+            device(turn),
+        )
+
+    def compute(inner):
+        buffer = buffers[inner]
+        head = group(0) * site_heads + inner
+        columns = slice(inner * head_size, (inner + 1) * head_size)
+
+        def pooled(kind):
+            cubes = buffer[:, kind].astype(jnp.float32)
+            return (jnp.sum(cubes, axis=1) * (1.0 / CUBE)).astype(jnp.bfloat16)
+
+        pooled_keys = pooled(0)
+        pooled_values = pooled(1)
+
+        def softmax(queries, keys, values):
+            scores = (
+                lax.dot_general(
+                    queries, keys, (((1,), (1,)), ((), ())), preferred_element_type=jnp.float32
+                )
+                * factor
+            )
+            weights = jnp.exp(scores - jnp.max(scores, axis=1, keepdims=True))
+            total = jnp.sum(weights, axis=1, keepdims=True)
+            return (
+                jnp.dot(weights.astype(jnp.bfloat16), values, preferred_element_type=jnp.float32)
+                / total
+            )
+
+        def one_turn(turn, carry):
+            queries = query_ref[turn, :, columns]
+            coarse = softmax(queries, pooled_keys, pooled_values)
+            gates = gate_ref[turn].astype(jnp.float32)
+            lane = lax.broadcasted_iota(jnp.int32, gates.shape, 1)
+            coarse_gate = jax.nn.sigmoid(
+                jnp.sum(jnp.where(lane == head, gates, 0.0), axis=1, keepdims=True)
+            )
+            fine_gate = jax.nn.sigmoid(
+                jnp.sum(jnp.where(lane == head + head_count, gates, 0.0), axis=1, keepdims=True)
+            )
+            fine = []
+            for cube in range(local_cubes):
+                block = device(turn) * local_cubes + cube
+                base = (block * head_count + head) * picks
+                chosen = [position_ref[selection_ref[base + pick]] for pick in range(picks)]
+                keys = jnp.concatenate([buffer[t, 0] for t in chosen], axis=0)
+                values = jnp.concatenate([buffer[t, 1] for t in chosen], axis=0)
+                fine.append(softmax(queries[cube * CUBE : (cube + 1) * CUBE], keys, values))
+            fine = jnp.concatenate(fine, axis=0)
+            done[inner, turn] = (coarse_gate * coarse + fine_gate * fine).astype(done.dtype)
+            return carry
+
+        lax.fori_loop(0, SITES, one_turn, 0)
+        for turn in range(1, SITES):
+            out_copy(turn, inner).start()
+        out_block[:, head_columns(head, 1)] = done[inner, 0]
+
+    far_first = (7, 6, 5, 4, 3, 2, 1)
+
+    def send(inner):
+        for turn in range(SITES):
+            for copy in fills(turn, inner):
+                copy.wait()
+        for turn in far_first:
+            kv_copy(turn, inner).start()
+        pass_on(0, inner).start()
+
+    for copy in own_queries():
+        copy.start()
+    for inner in range(site_heads):
+        for turn in range(SITES):
+            for copy in fills(turn, inner):
+                copy.start()
+    barrier = pltpu.get_barrier_semaphore()
+    for partner in [sibling] + [device(turn) for turn in range(1, turns)]:
+        pl.semaphore_signal(
+            barrier, inc=1, device_id={"cubes": partner}, device_id_type=pl.DeviceIdType.MESH
+        )
+    pl.semaphore_wait(barrier, turns)
+    for copy in own_queries():
+        copy.wait()
+    for turn in range(1, SITES):
+        for copy in query_copies(turn):
+            copy.start()
+    for inner in range(min(LOOKAHEAD, site_heads)):
+        send(inner)
+    for inner in range(site_heads):
+        for turn in range(1, turns):
+            kv_arrival(turn, inner).wait_recv()
+            pass_on(turn, inner).start()
+        if inner + LOOKAHEAD < site_heads:
+            send(inner + LOOKAHEAD)
+        if inner == 0:
+            for turn in range(1, SITES):
+                for copy in query_copies(turn):
+                    copy.wait_recv()
+        for turn in range(turns):
+            passed_arrival(turn, inner).wait_recv()
+        compute(inner)
+    for inner in range(site_heads):
+        for turn in range(1, SITES):
+            out_arrival(turn, inner).wait_recv()
+    out_ref[...] = out_block[...]
+    for turn in range(1, SITES):
+        for copy in query_copies(turn):
+            copy.wait_send()
+    for inner in range(site_heads):
+        for turn in range(1, turns):
+            kv_copy(turn, inner).wait_send()
+        for turn in range(turns):
+            pass_on(turn, inner).wait_send()
+        for turn in range(1, SITES):
+            out_copy(turn, inner).wait_send()
+
+
+def gathered_body(query_rows, key_rows, value_rows, gate_logits, selection, cube_ids):
+    token_count, feature_width = query_rows.shape
+    head_count = gate_logits.shape[1] // 2
+    head_size = feature_width // head_count
+    local_cubes = token_count // CUBE
+    total_cubes = cube_ids.shape[0]
+    picks = selection.shape[2]
+    cube_range = jnp.arange(total_cubes, dtype=jnp.int32)
+    position = jnp.sum(
+        jnp.where(cube_ids[None, :] == cube_range[:, None], cube_range[None, :], 0), axis=1
+    )
+    site_heads = head_count // SITES
+    turns = SITES * HALVES
+    block = (local_cubes, 2, CUBE, head_size)
+    return pl.pallas_call(
+        functools.partial(attention_kernel, (head_count, head_size, local_cubes, picks)),
+        out_shape=jax.ShapeDtypeStruct((token_count, feature_width), jnp.bfloat16),
+        in_specs=[pl.BlockSpec(memory_space=pltpu.SMEM)] * 2
+        + [pl.BlockSpec(memory_space=pltpu.HBM)] * 4,
+        out_specs=pl.BlockSpec(memory_space=pltpu.VMEM),
+        scratch_shapes=[
+            pltpu.VMEM((total_cubes, 2, CUBE, head_size), jnp.bfloat16)
+            for unused in range(site_heads)
+        ]
+        + [
+            pltpu.VMEM((SITES - 1, site_heads) + block, jnp.bfloat16),
+            pltpu.VMEM((SITES, token_count, site_heads * head_size), jnp.bfloat16),
+            pltpu.VMEM((SITES,) + gate_logits.shape, jnp.bfloat16),
+            pltpu.VMEM((site_heads, SITES, token_count, head_size), jnp.bfloat16),
+            pltpu.VMEM((token_count, feature_width), jnp.bfloat16),
+            pltpu.SemaphoreType.DMA((site_heads, 2 * turns)),
+            pltpu.SemaphoreType.DMA((site_heads, 2 * turns)),
+            pltpu.SemaphoreType.DMA((2, SITES)),
+            pltpu.SemaphoreType.DMA((2, SITES)),
+            pltpu.SemaphoreType.DMA((site_heads, SITES)),
+            pltpu.SemaphoreType.DMA((site_heads, SITES)),
+            pltpu.SemaphoreType.DMA((SITES, site_heads, 2)),
+            pltpu.SemaphoreType.DMA((2,)),
+        ],
+        compiler_params=pltpu.CompilerParams(
+            collective_id=0, has_side_effects=True, vmem_limit_bytes=VMEM_GRANT
+        ),
+    )(
+        position,
+        selection.reshape(-1),
+        query_rows,
+        key_rows.reshape(local_cubes, CUBE, feature_width),
+        value_rows.reshape(local_cubes, CUBE, feature_width),
+        gate_logits,
+    )
+
+
+def body(query_rows, key_rows, value_rows, gate_logits, selection, cube_ids):
+    device_count = lax.axis_size("cubes")
+    head_count = gate_logits.shape[1] // 2
+    fits = (
+        device_count == CORES * SITES * HALVES
+        and grid_of(device_count) == (2 * HALVES, SITES // 2)
+        and head_count % SITES == 0
+    )
+    return (gathered_body if fits else streamed_body)(
+        query_rows, key_rows, value_rows, gate_logits, selection, cube_ids
+    )
+
 
 def solution(mesh):
     placed = (

time: 516 us -> 83.2 us (0.16)
  waiting for transfers between devices: 235 us -> 0 us
  Pallas kernels: 0 us -> 76.3 us
  starting transfers between devices: 76 us -> 0 us
  local copies, waits for them, and re-layouts: 61.1 us -> 5.87 us
  matrix products: 48.6 us -> 0 us
  other arithmetic: 48.2 us -> 0.65 us
  blocking collectives: 41.3 us -> 0 us
    all_to_all x11 -> x0, waiting for transfers between devices: 235 us -> none  [one_round(): lax.all_to_all(held_pairs(incoming), 'cubes', split_axis=0, concat_axis=0...]
    pallas_call x0 -> x1, Pallas kernels: none -> 76.3 us  [gathered_body(): pl.pallas_call(functools.partial(attention_kernel, (head_count, head_size...]
    all_to_all x11 -> x0, starting transfers between devices: 76 us -> none  [one_round(): lax.all_to_all(held_pairs(incoming), 'cubes', split_axis=0, concat_axis=0...]
    dot_general x46 -> x0, matrix products: 48.6 us -> none  [the longest x11 20.3 us: merge_slots(): jnp.dot(onehot, weighted, precision=lax.Precision.HIGHEST)]
    gather x36 -> x0, local copies, waits for them, and re-layouts: 44.7 us -> none  [the longest x11 21.3 us: held_pairs(): picked = jnp.take(pair_groups, source, axis=0)]
    all_gather x2 -> x0, blocking collectives: 41.3 us -> none  [the longest x1 23.3 us: body(): piece_keys = lax.all_gather(pooled_keys, 'cubes', axis=0, tiled=True)]
    gather x25 -> x0, other arithmetic: 21.8 us -> none  [the longest x3 21.6 us: body(): jnp.take(position, selection.reshape(-1))]
    select_n x23 -> x0, other arithmetic: 13.3 us -> none  [the longest x11 13.2 us: held_pairs(): jnp.where((incoming >= 0).reshape(-1)[:, None, None], picked, jnp.zeros((...]
  transfers between devices with their start and end apart: 11 -> 0, of which waited for: 11 -> 0; matrix products, arithmetic and copies ran while one was open for 3% -> 0% of each run, Pallas kernels for 0% -> 0%
where the time goes in v3:
time: 83.2 us; the launch traced here: 82.9 us
  Pallas kernels  76.3 us (92%)
  local copies, waits for them, and re-layouts  5.87 us (7%)
    pallas_call x1, Pallas kernels, gathered_body(): pl.pallas_call(functools.partial(attention_kernel, (head_count, head_size...  76.3 us
    unnamed x5, local copies, waits for them, and re-layouts  5.12 us

profile of v3, /device:TPU:0, one launch (start us, length us, event | category | flops | bytes accessed | tf_op | source)
XLA Modules:
  0.0 82.9 jit_solution(8010183022104494504)
XLA Ops:
  0.0 0.0 copy-start
  0.0 0.7 copy-done
  0.7 0.7 select_reduce_fusion.position_ref
  1.3 1.4 %copy.11.gate_rows = bf16[128,40]{1,0:T(8,128)(2,1)} copy(bf16[128,40]{0,1:T(8,128)(2,1)} %param.9) | data formatting | bytes 20480 | tf_op args[3]
  2.7 1.1 %copy.10 = s32[32,20,8]{2,1,0:T(8,128)S(1)} copy(s32[32,20,8]{0,2,1:T(8,128)} %param.10) | data formatting | bytes 40960 | tf_op args[4]
  3.8 0.7 reshape.10.selection_ref
  4.6 76.3 %shard_map.64 = bf16[128,2560]{1,0:T(8,128)(2,1)} custom-call(s32[32]{0:T(128)} %select_reduce_fusion.position_ref, s32[5120]{0:T(1024)} %reshape.10.selection_ref, bf16[128,2560]{1,0:T(8,128)(2,1)} %query_rows.1, bf16[2,64,2560]{2,1,0:T(8,128)(2,1)} %bitcast.2, bf16[2,64,2560]{2,1,0:T(8,128)(2,1)} %bitcast.3, bf16[128,40]{1,0:T(8,128)(2,1)} %copy.11.gate_rows), custom_call_target="tpu_custom_call" | custom-call | tf_op jit(solution)/shard_map/pallas_call | solution.py:471
  80.9 2.0 %copy.13 = bf16[128,2560]{1,0:T(8,128)(2,1)} copy(bf16[128,2560]{1,0:T(8,128)(2,1)} %shard_map.64) | data formatting | bytes 1310720
Async XLA Ops:
  0.0 0.7 copy-start

commit v4 on v3

--- a/solution.py
+++ b/solution.py
@@ -9,7 +9,7 @@
 from jax.sharding import PartitionSpec as P
 
 CUBE = 64
-LOOKAHEAD = 2
+LOOKAHEAD = 3
 
 
 NEG_START = -1e30
@@ -203,21 +203,23 @@
 
 def attention_kernel(
     sizes,
-    position_ref,
+    cube_ids_ref,
     selection_ref,
     query_rows,
     key_cubes,
     value_cubes,
-    gate_rows,
+    gate_columns,
     out_ref,
     *scratch,
 ):
     head_count, head_size, local_cubes, picks = sizes
     site_heads = head_count // SITES
     buffers = scratch[:site_heads]
-    (stage, query_ref, gate_ref, done, out_block) = scratch[site_heads : site_heads + 5]
+    (stage, query_ref, gate_turned, gate_ref, done, out_block, position_ref) = scratch[
+        site_heads : site_heads + 7
+    ]
     (kv_send, kv_recv, query_send, query_recv, out_send, out_recv, kv_local, query_local) = scratch[
-        site_heads + 5 :
+        site_heads + 7 :
     ]
     factor = 1.0 / math.sqrt(head_size)
     width = site_heads * head_size
@@ -273,7 +275,7 @@
         columns = head_columns(group(0) * site_heads, site_heads)
         return [
             pltpu.make_async_copy(query_rows.at[:, columns], query_ref.at[0], query_local.at[0]),
-            pltpu.make_async_copy(gate_rows, gate_ref.at[0], query_local.at[1]),
+            pltpu.make_async_copy(gate_columns, gate_turned, query_local.at[1]),
         ]
 
     def query_copies(turn):
@@ -368,7 +370,7 @@
                 / total
             )
 
-        def one_turn(turn, carry):
+        def one_turn(turn):
             queries = query_ref[turn, :, columns]
             coarse = softmax(queries, pooled_keys, pooled_values)
             gates = gate_ref[turn].astype(jnp.float32)
@@ -382,19 +384,23 @@
             fine = []
             for cube in range(local_cubes):
                 block = device(turn) * local_cubes + cube
-                base = (block * head_count + head) * picks
-                chosen = [position_ref[selection_ref[base + pick]] for pick in range(picks)]
+                chosen = [position_ref[selection_ref[head, pick, block]] for pick in range(picks)]
                 keys = jnp.concatenate([buffer[t, 0] for t in chosen], axis=0)
                 values = jnp.concatenate([buffer[t, 1] for t in chosen], axis=0)
                 fine.append(softmax(queries[cube * CUBE : (cube + 1) * CUBE], keys, values))
             fine = jnp.concatenate(fine, axis=0)
-            done[inner, turn] = (coarse_gate * coarse + fine_gate * fine).astype(done.dtype)
-            return carry
-
-        lax.fori_loop(0, SITES, one_turn, 0)
-        for turn in range(1, SITES):
-            out_copy(turn, inner).start()
-        out_block[:, head_columns(head, 1)] = done[inner, 0]
+            return (coarse_gate * coarse + fine_gate * fine).astype(done.dtype)
+
+        for pair in ((3, 2), (1, 0)):
+            results = [one_turn(turn) for turn in pair]
+            for turn, result in zip(pair, results):
+                if turn == 0:
+                    out_block[:, head_columns(head, 1)] = result
+                else:
+                    done[inner, turn] = result
+            for turn in pair:
+                if turn != 0:
+                    out_copy(turn, inner).start()
 
     far_first = (7, 6, 5, 4, 3, 2, 1)
 
@@ -420,11 +426,21 @@
     pl.semaphore_wait(barrier, turns)
     for copy in own_queries():
         copy.wait()
+    gate_ref[0] = gate_turned[...].astype(jnp.float32).T.astype(gate_ref.dtype)
     for turn in range(1, SITES):
         for copy in query_copies(turn):
             copy.start()
     for inner in range(min(LOOKAHEAD, site_heads)):
         send(inner)
+
+    def place(cube, carry):
+        found = jnp.int32(0)
+        for block in range(cube_ids_ref.shape[0]):
+            found = jnp.where(cube_ids_ref[block] == cube, block, found)
+        position_ref[cube] = found
+        return carry
+
+    lax.fori_loop(0, cube_ids_ref.shape[0], place, 0)
     for inner in range(site_heads):
         for turn in range(1, turns):
             kv_arrival(turn, inner).wait_recv()
@@ -461,10 +477,6 @@
     local_cubes = token_count // CUBE
     total_cubes = cube_ids.shape[0]
     picks = selection.shape[2]
-    cube_range = jnp.arange(total_cubes, dtype=jnp.int32)
-    position = jnp.sum(
-        jnp.where(cube_ids[None, :] == cube_range[:, None], cube_range[None, :], 0), axis=1
-    )
     site_heads = head_count // SITES
     turns = SITES * HALVES
     block = (local_cubes, 2, CUBE, head_size)
@@ -481,9 +493,11 @@
         + [
             pltpu.VMEM((SITES - 1, site_heads) + block, jnp.bfloat16),
             pltpu.VMEM((SITES, token_count, site_heads * head_size), jnp.bfloat16),
+            pltpu.VMEM(gate_logits.shape[::-1], jnp.bfloat16),
             pltpu.VMEM((SITES,) + gate_logits.shape, jnp.bfloat16),
             pltpu.VMEM((site_heads, SITES, token_count, head_size), jnp.bfloat16),
             pltpu.VMEM((token_count, feature_width), jnp.bfloat16),
+            pltpu.SMEM((total_cubes,), jnp.int32),
             pltpu.SemaphoreType.DMA((site_heads, 2 * turns)),
             pltpu.SemaphoreType.DMA((site_heads, 2 * turns)),
             pltpu.SemaphoreType.DMA((2, SITES)),
@@ -497,12 +511,12 @@
             collective_id=0, has_side_effects=True, vmem_limit_bytes=VMEM_GRANT
         ),
     )(
-        position,
-        selection.reshape(-1),
+        cube_ids,
+        selection.transpose(1, 2, 0),
         query_rows,
         key_rows.reshape(local_cubes, CUBE, feature_width),
         value_rows.reshape(local_cubes, CUBE, feature_width),
-        gate_logits,
+        gate_logits.T,
     )
 
 

time: 83.2 us -> 78.5 us (0.944)
  local copies, waits for them, and re-layouts: 5.87 us -> 1.97 us
    unnamed x5 -> x1, local copies, waits for them, and re-layouts: 5.12 us -> 1.97 us
where the time goes in v4:
time: 78.5 us; the launch traced here: 78.3 us
  Pallas kernels  76.3 us (97%)
  local copies, waits for them, and re-layouts  1.97 us (3%)
    pallas_call x1, Pallas kernels, gathered_body(): pl.pallas_call(functools.partial(attention_kernel, (head_count, head_size...  76.3 us
    unnamed x1, local copies, waits for them, and re-layouts  1.97 us

profile of v4, /device:TPU:0, one launch (start us, length us, event | category | flops | bytes accessed | tf_op | source)
XLA Modules:
  0.0 78.3 jit_solution(13995110137628554153)
XLA Ops:
  0.0 76.3 %shard_map.64 = bf16[128,2560]{1,0:T(8,128)(2,1)} custom-call(s32[32]{0:T(128)} %cube_ids_ref.1, s32[20,8,32]{2,1,0:T(8,128)} %bitcast.6, bf16[128,2560]{1,0:T(8,128)(2,1)} %query_rows.1, bf16[2,64,2560]{2,1,0:T(8,128)(2,1)} %bitcast.4, bf16[2,64,2560]{2,1,0:T(8,128)(2,1)} %bitcast.5, bf16[40,128]{1,0:T(8,128)(2,1)} %bitcast.7), custom_call_target="tpu_custom_call" | custom-call | tf_op jit(solution)/shard_map/pallas_call | solution.py:483
  76.3 2.0 %copy.8 = bf16[128,2560]{1,0:T(8,128)(2,1)} copy(bf16[128,2560]{1,0:T(8,128)(2,1)} %shard_map.64) | data formatting | bytes 1310720

commit v5 on v4

--- a/solution.py
+++ b/solution.py
@@ -9,7 +9,7 @@
 from jax.sharding import PartitionSpec as P
 
 CUBE = 64
-LOOKAHEAD = 3
+LOOKAHEAD = 2
 
 
 NEG_START = -1e30
@@ -221,8 +221,7 @@
     (kv_send, kv_recv, query_send, query_recv, out_send, out_recv, kv_local, query_local) = scratch[
         site_heads + 7 :
     ]
-    factor = 1.0 / math.sqrt(head_size)
-    width = site_heads * head_size
+    factor = math.log2(math.e) / math.sqrt(head_size)
     me = lax.axis_index("cubes")
     core = me % CORES
     x = (me // CORES) % 2
@@ -325,20 +324,18 @@
         return remote(region, region, kv_send.at[inner, slot], kv_recv.at[inner, slot], sibling)
 
     def out_copy(turn, inner):
-        columns = head_columns(group(0) * site_heads + inner, 1)
         return remote(
             done.at[inner, turn],
-            out_block.at[:, columns],
+            out_block.at[:, head_columns(group(0) * site_heads + inner, 1)],
             out_send.at[inner, turn],
             out_recv.at[inner, turn],
             device(turn),
         )
 
     def out_arrival(turn, inner):
-        columns = head_columns(group(turn) * site_heads + inner, 1)
         return remote(
             done.at[inner, turn],
-            out_block.at[:, columns],
+            out_block.at[:, head_columns(group(turn) * site_heads + inner, 1)],
             out_send.at[inner, turn],
             out_recv.at[inner, turn],
             device(turn),
@@ -357,13 +354,10 @@
         pooled_values = pooled(1)
 
         def softmax(queries, keys, values):
-            scores = (
-                lax.dot_general(
-                    queries, keys, (((1,), (1,)), ((), ())), preferred_element_type=jnp.float32
-                )
-                * factor
+            scores = lax.dot_general(
+                queries, keys, (((1,), (1,)), ((), ())), preferred_element_type=jnp.float32
             )
-            weights = jnp.exp(scores - jnp.max(scores, axis=1, keepdims=True))
+            weights = jnp.exp2((scores - jnp.max(scores, axis=1, keepdims=True)) * factor)
             total = jnp.sum(weights, axis=1, keepdims=True)
             return (
                 jnp.dot(weights.astype(jnp.bfloat16), values, preferred_element_type=jnp.float32)
@@ -441,12 +435,18 @@
         return carry
 
     lax.fori_loop(0, cube_ids_ref.shape[0], place, 0)
+    for inner in range(min(LOOKAHEAD, site_heads), site_heads):
+        for turn in range(SITES):
+            for copy in fills(turn, inner):
+                copy.wait()
     for inner in range(site_heads):
         for turn in range(1, turns):
             kv_arrival(turn, inner).wait_recv()
             pass_on(turn, inner).start()
+            if inner + LOOKAHEAD < site_heads:
+                kv_copy(turn, inner + LOOKAHEAD).start()
         if inner + LOOKAHEAD < site_heads:
-            send(inner + LOOKAHEAD)
+            pass_on(0, inner + LOOKAHEAD).start()
         if inner == 0:
             for turn in range(1, SITES):
                 for copy in query_copies(turn):
@@ -457,7 +457,7 @@
     for inner in range(site_heads):
         for turn in range(1, SITES):
             out_arrival(turn, inner).wait_recv()
-    out_ref[...] = out_block[...]
+    out_ref[...] = out_block[...].astype(out_ref.dtype)
     for turn in range(1, SITES):
         for copy in query_copies(turn):
             copy.wait_send()
@@ -480,9 +480,9 @@
     site_heads = head_count // SITES
     turns = SITES * HALVES
     block = (local_cubes, 2, CUBE, head_size)
-    return pl.pallas_call(
+    mixed = pl.pallas_call(
         functools.partial(attention_kernel, (head_count, head_size, local_cubes, picks)),
-        out_shape=jax.ShapeDtypeStruct((token_count, feature_width), jnp.bfloat16),
+        out_shape=jax.ShapeDtypeStruct((token_count, feature_width), jnp.float32),
         in_specs=[pl.BlockSpec(memory_space=pltpu.SMEM)] * 2
         + [pl.BlockSpec(memory_space=pltpu.HBM)] * 4,
         out_specs=pl.BlockSpec(memory_space=pltpu.VMEM),
@@ -518,6 +518,7 @@
         value_rows.reshape(local_cubes, CUBE, feature_width),
         gate_logits.T,
     )
+    return mixed.astype(jnp.bfloat16)
 
 
 def body(query_rows, key_rows, value_rows, gate_logits, selection, cube_ids):

time: 78.5 us -> 78.8 us (level)
  other arithmetic: 0 us -> 2.22 us
  local copies, waits for them, and re-layouts: 1.97 us -> 0 us
    convert_element_type x0 -> x1, other arithmetic: none -> 2.22 us  [gathered_body(): return mixed.astype(jnp.bfloat16)]
    unnamed x1 -> x0, local copies, waits for them, and re-layouts: 1.97 us -> none
where the time goes in v5:
time: 78.8 us; the launch traced here: 78.6 us
  Pallas kernels  76.4 us (97%)
  other arithmetic  2.22 us (3%)
    pallas_call x1, Pallas kernels, gathered_body(): pl.pallas_call(functools.partial(attention_kernel, (head_count, head_size...  76.4 us
    convert_element_type x1, other arithmetic, gathered_body(): return mixed.astype(jnp.bfloat16)  2.22 us

profile of v5, /device:TPU:0, one launch (start us, length us, event | category | flops | bytes accessed | tf_op | source)
XLA Modules:
  0.0 78.6 jit_solution(16097993989720842165)
XLA Ops:
  0.0 76.4 %shard_map.64 = f32[128,2560]{1,0:T(8,128)} custom-call(s32[32]{0:T(128)} %cube_ids_ref.1, s32[20,8,32]{2,1,0:T(8,128)} %bitcast.6, bf16[128,2560]{1,0:T(8,128)(2,1)} %query_rows.1, bf16[2,64,2560]{2,1,0:T(8,128)(2,1)} %bitcast.4, bf16[2,64,2560]{2,1,0:T(8,128)(2,1)} %bitcast.5, bf16[40,128]{1,0:T(8,128)(2,1)} %bitcast.7), custom_call_target="tpu_custom_call" | custom-call | tf_op jit(solution)/shard_map/pallas_call | solution.py:483
  76.4 2.2 %convert_element_type.3 = bf16[128,2560]{1,0:T(8,128)(2,1)} convert(f32[128,2560]{1,0:T(8,128)} %shard_map.64) | non-fusion elementwise | flops 327680 | bytes 1966080 | tf_op jit(solution)/shard_map/convert_element_type | solution.py:521

commit v6 on v4

--- a/solution.py
+++ b/solution.py
@@ -9,7 +9,7 @@
 from jax.sharding import PartitionSpec as P
 
 CUBE = 64
-LOOKAHEAD = 3
+LOOKAHEAD = 5
 
 
 NEG_START = -1e30

time: 78.5 us -> 78.5 us (level)
  no operation moved by 1% of the time
where the time goes in v6:
time: 78.5 us; the launch traced here: 78.3 us
  Pallas kernels  76.3 us (97%)
  local copies, waits for them, and re-layouts  1.97 us (3%)
    pallas_call x1, Pallas kernels, gathered_body(): pl.pallas_call(functools.partial(attention_kernel, (head_count, head_size...  76.3 us
    unnamed x1, local copies, waits for them, and re-layouts  1.97 us

profile of v6, /device:TPU:0, one launch (start us, length us, event | category | flops | bytes accessed | tf_op | source)
XLA Modules:
  0.0 78.3 jit_solution(16106647838133766152)
XLA Ops:
  0.0 76.3 %shard_map.64 = bf16[128,2560]{1,0:T(8,128)(2,1)} custom-call(s32[32]{0:T(128)} %cube_ids_ref.1, s32[20,8,32]{2,1,0:T(8,128)} %bitcast.6, bf16[128,2560]{1,0:T(8,128)(2,1)} %query_rows.1, bf16[2,64,2560]{2,1,0:T(8,128)(2,1)} %bitcast.4, bf16[2,64,2560]{2,1,0:T(8,128)(2,1)} %bitcast.5, bf16[40,128]{1,0:T(8,128)(2,1)} %bitcast.7), custom_call_target="tpu_custom_call" | custom-call | tf_op jit(solution)/shard_map/pallas_call | solution.py:483
  76.3 2.0 %copy.8 = bf16[128,2560]{1,0:T(8,128)(2,1)} copy(bf16[128,2560]{1,0:T(8,128)(2,1)} %shard_map.64) | data formatting | bytes 1310720
